TPU v7x, 256 devices: a whole 4x4x8 slice. The times are simulated.
256 devices in a mesh: wide: 128 (over y, z, x_lo, core), row: 2 (over x_hi).
Axes of the slice: x: 4 (x_hi: 2, x_lo: 2; x = x_hi * 2 + x_lo), y: 4, z: 8, core: 2. Of those that a mesh axis runs over, the one named last changes fastest.
Arguments:
- pair: bfloat16 [512, 512, 128], P('wide', 'row'), may hold values from -6 to 6
- token_valid: int32 [512], replicated, may hold values 0 or 1
- w_pair: bfloat16 [128, 512], replicated, may hold values from -0.5 to 0.5
- w_gate: bfloat16 [128, 128], replicated, may hold values from -0.5 to 0.5
- w_out: bfloat16 [128, 128], replicated, may hold values from -0.5 to 0.5
Outputs:
- update: bfloat16 [512, 512, 128], P('wide', 'row')
All inputs are finite; a program needn't handle non-finite values.
Results may differ from a plain program's by a relative error of at most 0.017.
Values may be sent and summed in bfloat16 or wider, within the bound.
No kernel may reach another device: no remote copies, remote signals or barrier semaphores. Data moves between devices by JAX's collectives and lax.ppermute only.
A program may use at most 64 MiB of HBM per device.

v0:
```python
import jax
import jax.numpy as jnp
from jax import lax
from jax.sharding import PartitionSpec as P


def normalize(values, axis):
    mean = jnp.mean(values, axis=axis, keepdims=True)
    centered = values - mean
    spread = jnp.mean(centered * centered, axis=axis, keepdims=True)
    return centered * lax.rsqrt(spread + 1e-05)


def send_planes(left, right):
    return (
        lax.all_to_all(left, "wide", split_axis=0, concat_axis=1, tiled=True),
        lax.all_to_all(right, "wide", split_axis=0, concat_axis=1, tiled=True),
    )


def return_rows(product):
    return lax.all_to_all(
        lax.all_to_all(product, "row", split_axis=2, concat_axis=0, tiled=True),
        "wide",
        split_axis=0,
        concat_axis=1,
        tiled=True,
    )


def project_part(normed, weights, first, count):
    return jnp.einsum(
        "rqd,de->erq", normed, weights[:, first : first + count], preferred_element_type=jnp.float32
    )


def shards(pair, token_valid, w_pair, w_gate, w_out):
    rows_dev, cols_dev, width = pair.shape
    hidden = w_out.shape[0]
    valid = token_valid.astype(jnp.float32)
    row_valid = lax.dynamic_slice_in_dim(valid, lax.axis_index("wide") * rows_dev, rows_dev, 0)
    col_valid = lax.dynamic_slice_in_dim(valid, lax.axis_index("row") * cols_dev, cols_dev, 0)
    weight_mask = row_valid[:, None] * col_valid[None, :]
    normed = normalize(pair.astype(jnp.float32), 2).astype(jnp.bfloat16)
    left = (
        jax.nn.sigmoid(project_part(normed, w_pair, 0, hidden))
        * project_part(normed, w_pair, hidden, hidden)
        * weight_mask
    ).astype(jnp.bfloat16)
    right = (
        jax.nn.sigmoid(project_part(normed, w_pair, 2 * hidden, hidden))
        * project_part(normed, w_pair, 3 * hidden, hidden)
        * weight_mask
    ).astype(jnp.bfloat16)
    gating = jax.nn.sigmoid(
        jnp.einsum("rqd,de->rqe", normed, w_gate, preferred_element_type=jnp.float32)
    )
    left_plane, right_plane = send_planes(left, right)
    left_rows = lax.all_to_all(left_plane, "row", split_axis=1, concat_axis=2, tiled=True)
    summed = jnp.einsum(
        "cik,cjk->icj",
        left_rows,
        lax.all_gather(right_plane, "row", axis=2, tiled=True),
        preferred_element_type=jnp.float32,
    )
    returned = return_rows(summed.astype(jnp.bfloat16))
    tri_norm = normalize(returned.astype(jnp.float32), 1).astype(jnp.bfloat16)
    mixed = jnp.einsum("rhq,hc->rqc", tri_norm, w_out, preferred_element_type=jnp.float32)
    return (gating * mixed).astype(jnp.bfloat16)


def solution(mesh):
    placed = (P("wide", "row", None), P(), P(), P(), P())
    return jax.shard_map(
        shards, mesh=mesh, in_specs=placed, out_specs=P("wide", "row", None), check_vma=False
    )
```

profile of v0, /device:TPU:1, one launch (start us, length us, event | category | flops | bytes accessed | tf_op | source)
XLA Modules:
  0.0 108.3 jit_solution(8822140752811184442)
XLA Ops:
  0.0 0.0 copy-start
  0.0 0.0 copy-start.1
  0.0 0.7 convert_element_type.44
  0.7 0.1 dynamic_slice.6
  0.8 0.1 dynamic_slice.7
  0.9 1.1 %convert_reduce_fusion = f32[4,256]{1,0:T(4,128)S(1)} fusion(bf16[4,256,128]{2,1,0:T(8,128)(2,1)} %param.5), kind=kLoop, calls=%fused_computation.25 | loop fusion | flops 261120 | bytes 266240 | tf_op jit(solution)/shard_map/reduce_sum | solution.py:8
  2.0 0.0 copy-done.1
  2.0 0.0 copy-start.2
  2.0 0.4 fusion.19
  2.4 0.1 add_rsqrt_fusion.1
  2.5 0.4 copy-done.2
  2.9 0.5 fusion.2
  3.4 0.5 fusion.16
  3.9 0.9 copy.18
  4.8 14.9 %all-to-all-start.1 = ((bf16[128,4,256]{2,1,0:T(4,128)(2,1)}), bf16[128,4,256]{2,1,0:T(4,128)(2,1)S(1)}, u32[]{:S(2)}, u32[]{:S(2)}) async-start(bf16[128,4,256]{2,1,0:T(4,128)(2,1)} %copy.18), calls=%async_computation.1 | async-start | bytes 524288 | tf_op jit(solution)/shard_map/all_to_all | solution.py:16
  19.6 0.5 fusion.5
  20.1 0.5 fusion.15
  20.6 0.9 copy.17
  21.5 12.4 %all-to-all-done.1 = bf16[128,4,256]{2,1,0:T(4,128)(2,1)S(1)} async-done(((bf16[128,4,256]{2,1,0:T(4,128)(2,1)}), bf16[128,4,256]{2,1,0:T(4,128)(2,1)S(1)}, u32[]{:S(2)}, u32[]{:S(2)}) %all-to-all-start.1) | async-done | bytes 262176 | tf_op jit(solution)/shard_map/all_to_all | solution.py:16
  33.9 5.5 %all-to-all-start = ((bf16[128,4,256]{2,1,0:T(4,128)(2,1)}), bf16[128,4,256]{2,1,0:T(4,128)(2,1)S(1)}, u32[]{:S(2)}, u32[]{:S(2)}) async-start(bf16[128,4,256]{2,1,0:T(4,128)(2,1)} %copy.17), calls=%async_computation | async-start | bytes 524288 | tf_op jit(solution)/shard_map/all_to_all | solution.py:17
  39.4 0.2 all_to_all.61
  39.6 0.6 broadcast.80
  40.2 2.2 %reduce.1 = bf16[512,256]{1,0:T(8,128)(2,1)S(1)} reduce(bf16[512,1,256]{2,1,0:T(2,128)(2,1)S(1)} %bitcast.60, bf16[]{:T(256)} %broadcast.80), dimensions={1}, to_apply=%bitcast.50.reduce_sub_computation | reduce | bytes 524290
  42.4 0.8 reshape.78
  43.1 10.7 %all-to-all-done = bf16[128,4,256]{2,1,0:T(4,128)(2,1)S(1)} async-done(((bf16[128,4,256]{2,1,0:T(4,128)(2,1)}), bf16[128,4,256]{2,1,0:T(4,128)(2,1)S(1)}, u32[]{:S(2)}, u32[]{:S(2)}) %all-to-all-start) | async-done | bytes 262176 | tf_op jit(solution)/shard_map/all_to_all | solution.py:17
  53.8 3.7 %all-to-all-start.2 = ((bf16[2,2,32768]{2,1,0:T(2,128)(2,1)}), bf16[2,2,32768]{2,1,0:T(2,128)(2,1)S(1)}, u32[]{:S(2)}, u32[]{:S(2)}) async-start(bf16[2,2,32768]{2,1,0:T(2,128)(2,1)} %reshape.78), calls=%async_computation.2 | async-start | bytes 524288 | tf_op jit(solution)/shard_map/all_to_all | solution.py:59
  57.5 0.1 all_to_all.50
  57.6 11.7 %all_gather.3 = bf16[1,512,512]{2,1,0:T(8,128)(2,1)S(1)} all-gather(bf16[1,512,256]{2,1,0:T(8,128)(2,1)S(1)} %all_to_all.50), channel_id=1, replica_groups=mesh['wide'=128,'row'=2] {'row'}, dimensions={2}, use_global_device_ids=true | all-gather | bytes 786432 | tf_op jit(solution)/shard_map/all_gather | solution.py:63
  69.3 0.0 all-to-all-done.2
  69.3 0.3 reshape.79
  69.6 0.1 copy.20
  69.8 0.3 fusion.14
  70.1 0.4 copy.36
  70.5 2.2 %reduce.2 = bf16[512,256]{1,0:T(8,128)(2,1)S(1)} reduce(bf16[512,1,256]{2,1,0:T(2,128)(2,1)S(1)} %bitcast.61, bf16[]{:T(256)} %broadcast.80), dimensions={1}, to_apply=%bitcast.56.reduce_sub_computation | reduce | bytes 524290
  72.7 0.1 reshape.80
  72.7 7.9 %all_to_all.67 = bf16[2,2,32768]{2,1,0:T(2,128)(2,1)S(1)} all-to-all(bf16[2,2,32768]{2,1,0:T(2,128)(2,1)S(1)} %reshape.80), channel_id=1, replica_groups=mesh['wide'=128,'row'=2] {'row'}, dimensions={0} | all-to-all | bytes 524288 | tf_op jit(solution)/shard_map/all_to_all | solution.py:23
  80.7 0.3 reshape.81
  81.0 0.1 copy.22
  81.1 0.8 reduce.3
  81.9 0.9 reshape.82
  82.8 8.0 %all-to-all-start.4 = ((bf16[128,2,512]{2,1,0:T(2,128)(2,1)}), bf16[128,2,512]{2,1,0:T(2,128)(2,1)S(1)}, u32[]{:S(2)}, u32[]{:S(2)}) async-start(bf16[128,2,512]{2,1,0:T(2,128)(2,1)} %reshape.82), calls=%async_computation.4 | async-start | bytes 524288 | tf_op jit(solution)/shard_map/all_to_all | solution.py:22
  90.8 0.0 copy-done
  90.8 0.7 fusion.8
  91.5 13.7 %all-to-all-done.4 = bf16[128,2,512]{2,1,0:T(2,128)(2,1)S(1)} async-done(((bf16[128,2,512]{2,1,0:T(2,128)(2,1)}), bf16[128,2,512]{2,1,0:T(2,128)(2,1)S(1)}, u32[]{:S(2)}, u32[]{:S(2)}) %all-to-all-start.4) | async-done | bytes 262176 | tf_op jit(solution)/shard_map/all_to_all | solution.py:22
  105.1 0.2 reshape.83
  105.4 0.5 convert_bitcast_fusion
  105.9 0.5 fusion.33
  106.4 0.2 multiply_reduce_fusion
  106.6 0.0 copy-start.3
  106.6 0.1 multiply_convert_fusion
  106.8 0.6 copy-done.3
  107.4 1.0 fusion.13
  (5 shorter events, 0.1 us)
Async XLA Ops:
  0.0 90.8 %copy-start = (bf16[128,128]{1,0:T(8,128)(2,1)S(1)}, bf16[128,128]{1,0:T(8,128)(2,1)}, u32[]{:S(2)}) copy-start(bf16[128,128]{1,0:T(8,128)(2,1)} %param.8) | copy-start | bytes 98308
  0.0 2.0 %copy-start.1 = (bf16[4,256,128]{2,1,0:T(8,128)(2,1)S(1)}, bf16[4,256,128]{2,1,0:T(8,128)(2,1)}, u32[]{:S(2)}) copy-start(bf16[4,256,128]{2,1,0:T(8,128)(2,1)} %param.5) | copy-start | bytes 786436
  2.0 0.9 copy-start.2
  4.8 29.2 %all-to-all-start.1 = ((bf16[128,4,256]{2,1,0:T(4,128)(2,1)}), bf16[128,4,256]{2,1,0:T(4,128)(2,1)S(1)}, u32[]{:S(2)}, u32[]{:S(2)}) async-start(bf16[128,4,256]{2,1,0:T(4,128)(2,1)} %copy.18), calls=%async_computation.1 | async-start | bytes 524288 | tf_op jit(solution)/shard_map/all_to_all | solution.py:16
  33.9 19.9 %all-to-all-start = ((bf16[128,4,256]{2,1,0:T(4,128)(2,1)}), bf16[128,4,256]{2,1,0:T(4,128)(2,1)S(1)}, u32[]{:S(2)}, u32[]{:S(2)}) async-start(bf16[128,4,256]{2,1,0:T(4,128)(2,1)} %copy.17), calls=%async_computation | async-start | bytes 524288 | tf_op jit(solution)/shard_map/all_to_all | solution.py:17
  53.8 15.5 %all-to-all-start.2 = ((bf16[2,2,32768]{2,1,0:T(2,128)(2,1)}), bf16[2,2,32768]{2,1,0:T(2,128)(2,1)S(1)}, u32[]{:S(2)}, u32[]{:S(2)}) async-start(bf16[2,2,32768]{2,1,0:T(2,128)(2,1)} %reshape.78), calls=%async_computation.2 | async-start | bytes 524288 | tf_op jit(solution)/shard_map/all_to_all | solution.py:59
  82.8 22.4 %all-to-all-start.4 = ((bf16[128,2,512]{2,1,0:T(2,128)(2,1)}), bf16[128,2,512]{2,1,0:T(2,128)(2,1)S(1)}, u32[]{:S(2)}, u32[]{:S(2)}) async-start(bf16[128,2,512]{2,1,0:T(2,128)(2,1)} %reshape.82), calls=%async_computation.4 | async-start | bytes 524288 | tf_op jit(solution)/shard_map/all_to_all | solution.py:22
  106.6 0.8 copy-start.3
where the time goes:
time: 109 us; the launch traced here: 108 us
  waiting for transfers between devices  36.8 us (34%)
  starting transfers between devices  32.1 us (29%)
  blocking collectives  19.6 us (18%)
  other arithmetic  8.81 us (8%)
  local copies, waits for them, and re-layouts  6.98 us (6%)
  matrix products  3.86 us (4%)
    all_to_all x1, starting transfers between devices, send_planes(): lax.all_to_all(left, 'wide', split_axis=0, concat_axis=1, tiled=True)  14.9 us
    all_to_all x1, waiting for transfers between devices, return_rows(): lax.all_to_all(lax.all_to_all(product, 'row', split_axis=2, concat_axis=0...  13.7 us
    all_to_all x1, waiting for transfers between devices, send_planes(): lax.all_to_all(left, 'wide', split_axis=0, concat_axis=1, tiled=True)  12.4 us
    all_gather x1, blocking collectives, shards(): lax.all_gather(right_plane, 'row', axis=2, tiled=True)  11.7 us
    all_to_all x1, waiting for transfers between devices, send_planes(): lax.all_to_all(right, 'wide', split_axis=0, concat_axis=1, tiled=True)  10.7 us
    all_to_all x1, starting transfers between devices, return_rows(): lax.all_to_all(lax.all_to_all(product, 'row', split_axis=2, concat_axis=0...  7.97 us
    all_to_all x1, blocking collectives, return_rows(): lax.all_to_all(product, 'row', split_axis=2, concat_axis=0, tiled=True)  7.92 us
    all_to_all x1, starting transfers between devices, send_planes(): lax.all_to_all(right, 'wide', split_axis=0, concat_axis=1, tiled=True)  5.49 us
  transfers between devices with their start and end apart: 4, of which 3 were waited for; matrix products, arithmetic and copies ran while one was open for 6% of the time, Pallas kernels for 0%

commit v1 on v0

v1 whole, which is shorter than its diff:
```python
import jax
import jax.numpy as jnp
from jax import lax
from jax.sharding import PartitionSpec as P


def normalize(values, axis):
    mean = jnp.mean(values, axis=axis, keepdims=True)
    centered = values - mean
    spread = jnp.mean(centered * centered, axis=axis, keepdims=True)
    return centered * lax.rsqrt(spread + 1e-05)


def chip_groups(wide, row):
    chips = wide // 2
    return [
        [(chip * 2 + core) * row + half for half in range(row) for chip in range(chips)]
        for core in range(2)
    ]


def exchange(blocks, groups):
    return lax.all_to_all(
        blocks, ("wide", "row"), split_axis=0, concat_axis=0, tiled=True, axis_index_groups=groups
    )


def make(wide, row):
    groups = chip_groups(wide, row)
    chips = wide // 2

    def shards(pair, token_valid, w_pair, w_gate, w_out):
        rows_dev, cols_dev, width = pair.shape
        hidden = w_out.shape[0]
        valid = token_valid.astype(jnp.float32)
        row_valid = lax.dynamic_slice_in_dim(
            valid, lax.axis_index("wide") * rows_dev, rows_dev, 0
        )
        col_valid = lax.dynamic_slice_in_dim(valid, lax.axis_index("row") * cols_dev, cols_dev, 0)
        weight_mask = (row_valid[:, None] * col_valid[None, :]).reshape(1, -1)
        normed = normalize(pair.astype(jnp.float32), 2).astype(jnp.bfloat16)
        normed = normed.reshape(-1, width)
        proj = jnp.einsum("de,nd->en", w_pair, normed, preferred_element_type=jnp.float32)
        left = jax.nn.sigmoid(proj[:hidden]) * proj[hidden : 2 * hidden] * weight_mask
        right = jax.nn.sigmoid(proj[2 * hidden : 3 * hidden]) * proj[3 * hidden :] * weight_mask
        sent = jnp.concatenate(
            [
                left.astype(jnp.bfloat16).reshape(hidden, rows_dev, cols_dev),
                right.astype(jnp.bfloat16).reshape(hidden, rows_dev, cols_dev),
            ],
            axis=1,
        )
        got = exchange(sent, groups).reshape(row, chips, 2, rows_dev, cols_dev)
        own_left = got[:, :, 0].reshape(row, chips * rows_dev, cols_dev)
        own_right = got[:, :, 1].reshape(row, chips * rows_dev, cols_dev)
        other_right = lax.ppermute(own_right, "wide", [(i, i ^ 1) for i in range(wide)])
        core = lax.axis_index("wide") % 2
        pairs = jnp.where(
            core == 0,
            jnp.stack([own_right, other_right]),
            jnp.stack([other_right, own_right]),
        )
        plane = jnp.einsum("rik,qrjk->iqj", own_left, pairs, preferred_element_type=jnp.float32)
        plane = plane.astype(jnp.bfloat16).reshape(chips, rows_dev, 2, row, chips // row, rows_dev)
        plane = plane.transpose(3, 0, 1, 4, 2, 5).reshape(row * chips, rows_dev, cols_dev)
        returned = exchange(plane, groups)
        gating = jax.nn.sigmoid(
            jnp.einsum("nd,de->ne", normed, w_gate, preferred_element_type=jnp.float32)
        )
        tri_norm = normalize(returned.astype(jnp.float32), 0).astype(jnp.bfloat16)
        mixed = jnp.einsum(
            "hn,hc->nc", tri_norm.reshape(hidden, -1), w_out, preferred_element_type=jnp.float32
        )
        return (gating * mixed).astype(jnp.bfloat16).reshape(rows_dev, cols_dev, width)

    return shards


def solution(mesh):
    placed = (P("wide", "row", None), P(), P(), P(), P())
    return jax.shard_map(
        make(mesh.shape["wide"], mesh.shape["row"]),
        mesh=mesh,
        in_specs=placed,
        out_specs=P("wide", "row", None),
        check_vma=False,
    )
```

time: 109 us -> 98.6 us (0.905)
  local copies, waits for them, and re-layouts: 6.98 us -> 32.7 us
  waiting for transfers between devices: 36.8 us -> 12.5 us
  starting transfers between devices: 32.1 us -> 10.3 us
  blocking collectives: 19.6 us -> 33.2 us
  other arithmetic: 8.81 us -> 6.4 us
  matrix products: 3.86 us -> 2 us
    all_to_all x1, blocking collectives: 7.92 us -> 33.2 us  [exchange(): lax.all_to_all(blocks, ('wide', 'row'), split_axis=0, concat_axis=0, tile...]
    all_to_all x4 -> x1, waiting for transfers between devices: 36.8 us -> 11.6 us  [exchange(): lax.all_to_all(blocks, ('wide', 'row'), split_axis=0, concat_axis=0, tile...]
    all_to_all x4 -> x1, starting transfers between devices: 32.1 us -> 7.59 us  [exchange(): lax.all_to_all(blocks, ('wide', 'row'), split_axis=0, concat_axis=0, tile...]
    reshape x0 -> x5, local copies, waits for them, and re-layouts: none -> 20.5 us  [the longest x1 19 us: shards(): plane.astype(jnp.bfloat16)]
    all_gather x1 -> x0, blocking collectives: 11.7 us -> none  [shards(): lax.all_gather(right_plane, 'row', axis=2, tiled=True)]
    transpose x0 -> x1, local copies, waits for them, and re-layouts: none -> 11.3 us  [shards(): plane.transpose(3, 0, 1, 4, 2, 5).reshape(row * chips, rows_dev, cols_dev)]
    unnamed x2 -> x1, other arithmetic: 4.37 us -> 0.07 us
    unnamed x17 -> x8, local copies, waits for them, and re-layouts: 4.17 us -> 0.05 us
  transfers between devices with their start and end apart: 4 -> 2, of which waited for: 3 -> 2; matrix products, arithmetic and copies ran while one was open for 6% -> 1% of each run, Pallas kernels for 0% -> 0%
where the time goes in v1:
time: 98.6 us; the launch traced here: 97.2 us
  blocking collectives  33.2 us (34%)
  local copies, waits for them, and re-layouts  32.7 us (33%)
  waiting for transfers between devices  12.5 us (13%)
  starting transfers between devices  10.3 us (10%)
  other arithmetic  6.4 us (6%)
  matrix products  2 us (2%)
    all_to_all x1, blocking collectives, exchange(): lax.all_to_all(blocks, ('wide', 'row'), split_axis=0, concat_axis=0, tile...  33.2 us
    reshape x1, local copies, waits for them, and re-layouts, shards(): plane.astype(jnp.bfloat16)  19 us
    all_to_all x1, waiting for transfers between devices, exchange(): lax.all_to_all(blocks, ('wide', 'row'), split_axis=0, concat_axis=0, tile...  11.6 us
    transpose x1, local copies, waits for them, and re-layouts, shards(): plane.transpose(3, 0, 1, 4, 2, 5).reshape(row * chips, rows_dev, cols_dev)  11.3 us
    all_to_all x1, starting transfers between devices, exchange(): lax.all_to_all(blocks, ('wide', 'row'), split_axis=0, concat_axis=0, tile...  7.59 us
    ppermute x1, starting transfers between devices, shards(): lax.ppermute(own_right, 'wide', [(i, i ^ 1) for i in range(wide)])  2.75 us
  transfers between devices with their start and end apart: 2, of which 2 were waited for; matrix products, arithmetic and copies ran while one was open for 1% of the time, Pallas kernels for 0%

profile of v1, /device:TPU:1, one launch (start us, length us, event | category | flops | bytes accessed | tf_op | source)
XLA Modules:
  0.0 97.2 jit_solution(18070440125143978190)
XLA Ops:
  0.0 0.0 copy-start
  0.0 0.7 convert_element_type.29
  0.7 0.1 dynamic_slice.6
  0.8 0.1 dynamic_slice.7
  0.9 0.1 multiply_bitcast_fusion
  1.0 1.1 %convert_reduce_fusion.1 = f32[4,256]{1,0:T(4,128)S(1)} fusion(bf16[4,256,128]{2,1,0:T(8,128)(2,1)} %param.5), kind=kLoop, calls=%fused_computation.13 | loop fusion | flops 261120 | bytes 266240 | tf_op jit(solution)/shard_map/reduce_sum | solution.py:8
  2.1 1.3 %fusion.11 = f32[4,256]{1,0:T(4,128)S(1)} fusion(bf16[4,256,128]{2,1,0:T(8,128)(2,1)} %param.5, f32[4,256]{1,0:T(4,128)S(1)} %broadcast_multiply_fusion.1), kind=kLoop, calls=%fused_computation.20 | loop fusion | flops 523264 | bytes 270336 | tf_op jit(solution)/shard_map/reduce_sum | solution.py:10
  3.4 1.3 %fusion.12 = bf16[4,256,128]{2,1,0:T(8,128)(2,1)S(1)} fusion(bf16[4,256,128]{2,1,0:T(8,128)(2,1)} %param.5, f32[4,256]{1,0:T(4,128)S(1)} %add_rsqrt_fusion.1, f32[4,256]{1,0:T(4,128)S(1)} %broadcast_multiply_fusion.1), kind=kLoop, calls=%fused_computation.21 | loop fusion | flops 524288 | bytes 532480 | tf_op jit(solution)/shard_map/convert_element_type | solution.py:41
  4.7 0.0 copy-done
  4.7 0.4 convolution_bitcast_fusion
  5.1 0.3 fusion.19
  5.4 0.2 copy.19
  5.6 0.2 copy.20
  5.8 0.3 pad_maximum_fusion
  6.1 33.2 %all_to_all.10 = bf16[128,8,256]{2,1,0:T(8,128)(2,1)S(1)} all-to-all(bf16[128,8,256]{2,1,0:T(8,128)(2,1)S(1)} %pad_maximum_fusion), channel_id=1, replica_groups={{0,4,8,12,16,20,24,28,32,36,40,44,48,52,56,60,64,68,72,76,80,84,88,92,9..., dimensions={0} | all-to-all | bytes 1048576 | tf_op jit(solution)/shard_map/all_to_all | solution.py:23
  39.2 0.1 copy.21
  39.4 0.3 copy.23
  39.7 2.8 %collective-permute-start = (bf16[2,256,256]{2,0,1:T(2,128)(2,1)S(1)}, bf16[2,256,256]{2,0,1:T(2,128)(2,1)S(1)}, u32[]{:S(2)}, u32[]{:S(2)}) collective-permute-start(bf16[2,256,256]{2,0,1:T(2,128)(2,1)S(1)} %bitcast.41), channel_id=1, source_target_pairs={{0,2},{2,0},{4,6},{6,4},{8,10},{10,8},{12,14},{14,12},{16,18},{18,... | collective-permute-start | bytes 786440 | tf_op jit(solution)/shard_map/ppermute | solution.py:56
  42.4 0.2 copy.22
  42.6 0.1 reshape.73
  42.7 0.9 collective-permute-done
  43.6 0.8 broadcast_select_fusion
  44.4 0.3 fusion.3
  44.7 19.0 %reshape.69 = bf16[64,4,2,2,32,4]{5,4,3,1,0,2:T(8,128)(2,1)} reshape(bf16[256,2,256]{2,0,1:T(8,128)(2,1)S(1)} %fusion.3) | data formatting | bytes 524288 | tf_op jit(solution)/shard_map/reshape | solution.py:64
  63.7 0.0 copy-start.2
  63.7 11.3 %copy.26 = bf16[2,64,4,32,2,4]{1,0,5,4,3,2:T(2,128)(2,1)S(1)} copy(bf16[2,64,4,32,2,4]{5,3,0,2,1,4:T(8,128)(2,1)} %bitcast.34) | data formatting | bytes 524288 | tf_op jit(solution)/shard_map/transpose | solution.py:65
  75.0 0.2 reshape.70
  75.2 0.9 copy.27
  76.1 0.0 copy-start.1
  76.1 7.6 %all-to-all-start.1 = ((bf16[128,4,256]{2,1,0:T(4,128)(2,1)}), bf16[128,4,256]{2,1,0:T(4,128)(2,1)S(1)}, u32[]{:S(2)}, u32[]{:S(2)}) async-start(bf16[128,4,256]{2,1,0:T(4,128)(2,1)} %copy.27), calls=%async_computation.1 | async-start | bytes 524288 | tf_op jit(solution)/shard_map/all_to_all | solution.py:23
  83.7 0.0 copy-done.2
  83.7 0.3 fusion.2
  84.0 11.6 %all-to-all-done.1 = bf16[128,4,256]{2,1,0:T(4,128)(2,1)S(1)} async-done(((bf16[128,4,256]{2,1,0:T(4,128)(2,1)}), bf16[128,4,256]{2,1,0:T(4,128)(2,1)S(1)}, u32[]{:S(2)}, u32[]{:S(2)}) %all-to-all-start.1) | async-done | bytes 262176 | tf_op jit(solution)/shard_map/all_to_all | solution.py:23
  95.7 0.2 convert_reduce_fusion
  95.8 0.2 fusion.9
  96.1 0.1 fusion.10
  96.3 0.0 copy-done.1
  96.3 1.0 fusion.4
  (7 shorter events, 0.1 us)
Async XLA Ops:
  0.0 4.7 %copy-start = (bf16[128,512]{1,0:T(8,128)(2,1)S(1)}, bf16[128,512]{1,0:T(8,128)(2,1)}, u32[]{:S(2)}) copy-start(bf16[128,512]{1,0:T(8,128)(2,1)} %param.7) | copy-start | bytes 393220
  39.7 3.9 %collective-permute-start = (bf16[2,256,256]{2,0,1:T(2,128)(2,1)S(1)}, bf16[2,256,256]{2,0,1:T(2,128)(2,1)S(1)}, u32[]{:S(2)}, u32[]{:S(2)}) collective-permute-start(bf16[2,256,256]{2,0,1:T(2,128)(2,1)S(1)} %bitcast.41), channel_id=1, source_target_pairs={{0,2},{2,0},{4,6},{6,4},{8,10},{10,8},{12,14},{14,12},{16,18},{18,... | collective-permute-start | bytes 786440 | tf_op jit(solution)/shard_map/ppermute | solution.py:56
  63.7 20.1 %copy-start.2 = (bf16[128,128]{1,0:T(8,128)(2,1)S(1)}, bf16[128,128]{1,0:T(8,128)(2,1)}, u32[]{:S(2)}) copy-start(bf16[128,128]{1,0:T(8,128)(2,1)} %param.8) | copy-start | bytes 98308
  76.1 20.1 %copy-start.1 = (bf16[128,128]{1,0:T(8,128)(2,1)S(1)}, bf16[128,128]{1,0:T(8,128)(2,1)}, u32[]{:S(2)}) copy-start(bf16[128,128]{1,0:T(8,128)(2,1)} %param.9) | copy-start | bytes 98308
  76.1 19.5 %all-to-all-start.1 = ((bf16[128,4,256]{2,1,0:T(4,128)(2,1)}), bf16[128,4,256]{2,1,0:T(4,128)(2,1)S(1)}, u32[]{:S(2)}, u32[]{:S(2)}) async-start(bf16[128,4,256]{2,1,0:T(4,128)(2,1)} %copy.27), calls=%async_computation.1 | async-start | bytes 524288 | tf_op jit(solution)/shard_map/all_to_all | solution.py:23

commit v2 on v1

--- a/solution.py
+++ b/solution.py
@@ -1,6 +1,8 @@
 import jax
 import jax.numpy as jnp
 from jax import lax
+from jax.experimental import pallas as pl
+from jax.experimental.pallas import tpu as pltpu
 from jax.sharding import PartitionSpec as P
 
 
@@ -25,9 +27,61 @@
     )
 
 
+def dot_rows(left, right):
+    return lax.dot_general(
+        left, right, (((1,), (1,)), ((), ())), preferred_element_type=jnp.float32
+    )
+
+
+def plane_kernel(core_ref, got_ref, other_ref, out_ref):
+    blocks, rows, cols = out_ref.shape
+    chips = blocks // 2
+    size = chips * rows
+
+    def flat(values):
+        return values.astype(jnp.float32).reshape(size, cols).astype(jnp.bfloat16)
+
+    own = jnp.zeros((size, size), jnp.float32)
+    other = jnp.zeros((size, size), jnp.float32)
+    for half in range(2):
+        part = pl.ds(half * chips, chips)
+        left = flat(got_ref[part, :rows, :])
+        own += dot_rows(left, flat(got_ref[part, rows:, :]))
+        other += dot_rows(left, flat(other_ref[part, :, :]))
+    own = own.astype(jnp.bfloat16)
+    other = other.astype(jnp.bfloat16)
+    source = lax.broadcasted_iota(jnp.int32, (cols, cols), 0)
+    target = lax.broadcasted_iota(jnp.int32, (cols, cols), 1)
+    seat = source % (cols // 2)
+    seat_core = jnp.where(source < cols // 2, core_ref[0], 1 - core_ref[0])
+    place = (seat // rows * 2 + seat_core) * rows + seat % rows
+    order = jnp.where(place == target, 1.0, 0.0).astype(jnp.bfloat16)
+    for half in range(2):
+        span = slice(half * (size // 2), (half + 1) * (size // 2))
+        both = jnp.concatenate([own[:, span], other[:, span]], axis=1)
+        placed = jnp.dot(both, order, preferred_element_type=jnp.float32)
+        out_ref[pl.ds(half * chips, chips), :, :] = placed.reshape(chips, rows, cols).astype(
+            jnp.bfloat16
+        )
+
+
+def plane_blocks(core, got, other):
+    blocks, rows, cols = other.shape
+    return pl.pallas_call(
+        plane_kernel,
+        out_shape=jax.ShapeDtypeStruct((blocks, rows, cols), jnp.bfloat16),
+        in_specs=[
+            pl.BlockSpec(memory_space=pltpu.SMEM),
+            pl.BlockSpec(memory_space=pltpu.VMEM),
+            pl.BlockSpec(memory_space=pltpu.VMEM),
+        ],
+        out_specs=pl.BlockSpec(memory_space=pltpu.VMEM),
+        compiler_params=pltpu.CompilerParams(vmem_limit_bytes=32 * 1024 * 1024),
+    )(core, got, other)
+
+
 def make(wide, row):
     groups = chip_groups(wide, row)
-    chips = wide // 2
 
     def shards(pair, token_valid, w_pair, w_gate, w_out):
         rows_dev, cols_dev, width = pair.shape
@@ -50,19 +104,12 @@
             ],
             axis=1,
         )
-        got = exchange(sent, groups).reshape(row, chips, 2, rows_dev, cols_dev)
-        own_left = got[:, :, 0].reshape(row, chips * rows_dev, cols_dev)
-        own_right = got[:, :, 1].reshape(row, chips * rows_dev, cols_dev)
-        other_right = lax.ppermute(own_right, "wide", [(i, i ^ 1) for i in range(wide)])
-        core = lax.axis_index("wide") % 2
-        pairs = jnp.where(
-            core == 0,
-            jnp.stack([own_right, other_right]),
-            jnp.stack([other_right, own_right]),
+        got = exchange(sent, groups)
+        other = lax.ppermute(
+            got[:, rows_dev:, :], "wide", [(i, i ^ 1) for i in range(wide)]
         )
-        plane = jnp.einsum("rik,qrjk->iqj", own_left, pairs, preferred_element_type=jnp.float32)
-        plane = plane.astype(jnp.bfloat16).reshape(chips, rows_dev, 2, row, chips // row, rows_dev)
-        plane = plane.transpose(3, 0, 1, 4, 2, 5).reshape(row * chips, rows_dev, cols_dev)
+        core = (lax.axis_index("wide") % 2).astype(jnp.int32).reshape(1)
+        plane = plane_blocks(core, got, other)
         returned = exchange(plane, groups)
         gating = jax.nn.sigmoid(
             jnp.einsum("nd,de->ne", normed, w_gate, preferred_element_type=jnp.float32)

time: 98.6 us -> 66.9 us (0.68)
  local copies, waits for them, and re-layouts: 32.7 us -> 0.72 us
  Pallas kernels: 0 us -> 1.2 us
    reshape x3 -> x0, local copies, waits for them, and re-layouts: 20.1 us -> none  [the longest x1 19 us: shards(): plane.astype(jnp.bfloat16)]
    transpose x1 -> x0, local copies, waits for them, and re-layouts: 11.3 us -> none  [shards(): plane.transpose(3, 0, 1, 4, 2, 5).reshape(row * chips, rows_dev, cols_dev)]
    pallas_call x0 -> x1, Pallas kernels: none -> 1.2 us  [plane_blocks(): pl.pallas_call(plane_kernel, out_shape=jax.ShapeDtypeStruct((blocks, rows...]
  transfers between devices with their start and end apart: 2 -> 2, of which waited for: 2 -> 2; matrix products, arithmetic and copies ran while one was open for 1% -> 0% of each run, Pallas kernels for 0% -> 0%
where the time goes in v2:
time: 66.9 us; the launch traced here: 65.6 us
  blocking collectives  33.2 us (50%)
  waiting for transfers between devices  12.8 us (19%)
  starting transfers between devices  10.3 us (15%)
  other arithmetic  5.64 us (8%)
  matrix products  1.65 us (2%)
  Pallas kernels  1.2 us (2%)
  local copies, waits for them, and re-layouts  0.72 us (1%)
    all_to_all x1, blocking collectives, exchange(): lax.all_to_all(blocks, ('wide', 'row'), split_axis=0, concat_axis=0, tile...  33.2 us
    all_to_all x1, waiting for transfers between devices, exchange(): lax.all_to_all(blocks, ('wide', 'row'), split_axis=0, concat_axis=0, tile...  11.6 us
    all_to_all x1, starting transfers between devices, exchange(): lax.all_to_all(blocks, ('wide', 'row'), split_axis=0, concat_axis=0, tile...  7.59 us
    ppermute x1, starting transfers between devices, shards(): lax.ppermute(got[:, rows_dev:, :], 'wide', [(i, i ^ 1) for i in range(wid...  2.75 us
    reduce_sum x2, other arithmetic, normalize(): spread = jnp.mean(centered * centered, axis=axis, keepdims=True)  1.55 us
  transfers between devices with their start and end apart: 2, of which 2 were waited for; matrix products, arithmetic and copies ran while one was open for 0% of the time, Pallas kernels for 0%

profile of v2, /device:TPU:1, one launch (start us, length us, event | category | flops | bytes accessed | tf_op | source)
XLA Modules:
  0.0 65.6 jit_solution(13162996105288742833)
XLA Ops:
  0.0 0.0 copy-start
  0.0 0.7 %convert_element_type.26 = f32[512]{0:T(512)S(1)} convert(s32[512]{0:T(512)} %param.6) | non-fusion elementwise | flops 512 | bytes 4096 | tf_op jit(solution)/shard_map/convert_element_type | solution.py:89
  0.7 0.1 dynamic_slice.6
  0.8 0.1 dynamic_slice.7
  0.9 0.1 multiply_bitcast_fusion
  1.0 1.1 %convert_reduce_fusion.1 = f32[4,256]{1,0:T(4,128)S(1)} fusion(bf16[4,256,128]{2,1,0:T(8,128)(2,1)} %param.5), kind=kLoop, calls=%fused_computation.10 | loop fusion | flops 261120 | bytes 266240 | tf_op jit(solution)/shard_map/reduce_sum | solution.py:10
  2.1 1.3 %fusion.10 = f32[4,256]{1,0:T(4,128)S(1)} fusion(bf16[4,256,128]{2,1,0:T(8,128)(2,1)} %param.5, f32[4,256]{1,0:T(4,128)S(1)} %broadcast_multiply_fusion.1), kind=kLoop, calls=%fused_computation.17 | loop fusion | flops 523264 | bytes 270336 | tf_op jit(solution)/shard_map/reduce_sum | solution.py:12
  3.4 1.3 %fusion.11 = bf16[4,256,128]{2,1,0:T(8,128)(2,1)S(1)} fusion(bf16[4,256,128]{2,1,0:T(8,128)(2,1)} %param.5, f32[4,256]{1,0:T(4,128)S(1)} %add_rsqrt_fusion.1, f32[4,256]{1,0:T(4,128)S(1)} %broadcast_multiply_fusion.1), kind=kLoop, calls=%fused_computation.18 | loop fusion | flops 524288 | bytes 532480 | tf_op jit(solution)/shard_map/convert_element_type | solution.py:95
  4.7 0.0 copy-done
  4.7 0.4 convolution_bitcast_fusion
  5.1 0.3 fusion.18
  5.4 0.2 copy.8
  5.6 0.2 copy.9
  5.8 0.0 copy-start.2
  5.8 0.3 pad_maximum_fusion
  6.1 33.2 %all_to_all.10.got_ref = bf16[128,8,256]{2,1,0:T(8,128)(2,1)S(1)} all-to-all(bf16[128,8,256]{2,1,0:T(8,128)(2,1)S(1)} %pad_maximum_fusion), channel_id=1, replica_groups={{0,4,8,12,16,20,24,28,32,36,40,44,48,52,56,60,64,68,72,76,80,84,88,92,9..., dimensions={0} | all-to-all | bytes 1048576 | tf_op jit(solution)/shard_map/all_to_all | solution.py:25
  39.3 0.1 slice.24
  39.4 2.8 %collective-permute-start = (bf16[128,4,256]{2,1,0:T(4,128)(2,1)S(1)}, bf16[128,4,256]{2,1,0:T(4,128)(2,1)S(1)}, u32[]{:S(2)}, u32[]{:S(2)}) collective-permute-start(bf16[128,4,256]{2,1,0:T(4,128)(2,1)S(1)} %slice.24), channel_id=1, source_target_pairs={{0,2},{2,0},{4,6},{6,4},{8,10},{10,8},{12,14},{14,12},{16,18},{18,... | collective-permute-start | bytes 786440 | tf_op jit(solution)/shard_map/ppermute | solution.py:108
  42.2 1.2 %collective-permute-done.other_ref = bf16[128,4,256]{2,1,0:T(4,128)(2,1)S(1)} collective-permute-done((bf16[128,4,256]{2,1,0:T(4,128)(2,1)S(1)}, bf16[128,4,256]{2,1,0:T(4,128)(2,1)S(1)}, u32[]{:S(2)}, u32[]{:S(2)}) %collective-permute-start) | collective-permute-done | bytes 262176 | tf_op jit(solution)/shard_map/ppermute | solution.py:108
  43.3 1.2 %shard_map.55 = bf16[128,4,256]{2,1,0:T(4,128)(2,1)} custom-call(s32[1]{0:T(128)} %bitcast.1.core_ref, bf16[128,8,256]{2,1,0:T(8,128)(2,1)S(1)} %all_to_all.10.got_ref, bf16[128,4,256]{2,1,0:T(4,128)(2,1)S(1)} %collective-permute-done.other_ref), custom_call_target="tpu_custom_call" | custom-call | tf_op jit(solution)/shard_map/pallas_call | solution.py:70
  44.5 0.0 copy-start.1
  44.5 7.6 %all-to-all-start.1 = ((bf16[128,4,256]{2,1,0:T(4,128)(2,1)}), bf16[128,4,256]{2,1,0:T(4,128)(2,1)S(1)}, u32[]{:S(2)}, u32[]{:S(2)}) async-start(bf16[128,4,256]{2,1,0:T(4,128)(2,1)} %shard_map.55), calls=%async_computation.1 | async-start | bytes 524288 | tf_op jit(solution)/shard_map/all_to_all | solution.py:25
  52.1 0.0 copy-done.2
  52.1 0.3 fusion.2
  52.4 11.6 %all-to-all-done.1 = bf16[128,4,256]{2,1,0:T(4,128)(2,1)S(1)} async-done(((bf16[128,4,256]{2,1,0:T(4,128)(2,1)}), bf16[128,4,256]{2,1,0:T(4,128)(2,1)S(1)}, u32[]{:S(2)}, u32[]{:S(2)}) %all-to-all-start.1) | async-done | bytes 262176 | tf_op jit(solution)/shard_map/all_to_all | solution.py:25
  64.0 0.2 convert_reduce_fusion
  64.2 0.2 fusion.8
  64.4 0.1 fusion.9
  64.6 0.0 copy-done.1
  64.6 1.0 %fusion.3 = bf16[1024,128]{1,0:T(8,128)(2,1)} fusion(f32[1024,128]{1,0:T(8,128)S(1)} %fusion.2, bf16[128,1024]{1,0:T(8,128)(2,1)S(1)} %bitcast.23, bf16[128,128]{1,0:T(8,128)(2,1)S(1)} %copy-done.1), kind=kOutput, calls=%fused_computation.6 | convolution fusion | flops 33816576 | bytes 1081344 | tf_op jit(solution)/shard_map/hn,hc->nc/dot_general | solution.py:118
  (6 shorter events, 0.1 us)
Async XLA Ops:
  0.0 4.7 %copy-start = (bf16[128,512]{1,0:T(8,128)(2,1)S(1)}, bf16[128,512]{1,0:T(8,128)(2,1)}, u32[]{:S(2)}) copy-start(bf16[128,512]{1,0:T(8,128)(2,1)} %param.7) | copy-start | bytes 393220
  5.8 46.3 %copy-start.2 = (bf16[128,128]{1,0:T(8,128)(2,1)S(1)}, bf16[128,128]{1,0:T(8,128)(2,1)}, u32[]{:S(2)}) copy-start(bf16[128,128]{1,0:T(8,128)(2,1)} %param.8) | copy-start | bytes 98308
  39.4 3.9 %collective-permute-start = (bf16[128,4,256]{2,1,0:T(4,128)(2,1)S(1)}, bf16[128,4,256]{2,1,0:T(4,128)(2,1)S(1)}, u32[]{:S(2)}, u32[]{:S(2)}) collective-permute-start(bf16[128,4,256]{2,1,0:T(4,128)(2,1)S(1)} %slice.24), channel_id=1, source_target_pairs={{0,2},{2,0},{4,6},{6,4},{8,10},{10,8},{12,14},{14,12},{16,18},{18,... | collective-permute-start | bytes 786440 | tf_op jit(solution)/shard_map/ppermute | solution.py:108
  44.5 20.1 %copy-start.1 = (bf16[128,128]{1,0:T(8,128)(2,1)S(1)}, bf16[128,128]{1,0:T(8,128)(2,1)}, u32[]{:S(2)}) copy-start(bf16[128,128]{1,0:T(8,128)(2,1)} %param.9) | copy-start | bytes 98308
  44.5 19.5 %all-to-all-start.1 = ((bf16[128,4,256]{2,1,0:T(4,128)(2,1)}), bf16[128,4,256]{2,1,0:T(4,128)(2,1)S(1)}, u32[]{:S(2)}, u32[]{:S(2)}) async-start(bf16[128,4,256]{2,1,0:T(4,128)(2,1)} %shard_map.55), calls=%async_computation.1 | async-start | bytes 524288 | tf_op jit(solution)/shard_map/all_to_all | solution.py:25

commit v3 on v2

--- a/solution.py
+++ b/solution.py
@@ -33,7 +33,60 @@
     )
 
 
-def plane_kernel(core_ref, got_ref, other_ref, out_ref):
+def sigmoid(values):
+    return 0.5 * jnp.tanh(0.5 * values) + 0.5
+
+
+def project_kernel(pair_ref, valid_ref, w_ref, sent_ref, normed_ref, held):
+    rows, cols, width = pair_ref.shape
+    hidden = sent_ref.shape[0]
+    ones = jnp.ones((width, width), jnp.bfloat16)
+
+    def total(values):
+        return jnp.dot(values, ones, preferred_element_type=jnp.float32)
+
+    turned = w_ref[...].T
+    valid = valid_ref[...].astype(jnp.float32)
+    seat = lax.broadcasted_iota(jnp.int32, valid.shape, 1)
+    first = lax.axis_index("wide") * rows
+    col_valid = jnp.where(lax.axis_index("row") == 0, valid[:, :cols], valid[:, cols:])
+    for row in range(rows):
+        row_valid = jnp.sum(jnp.where(seat == first + row, valid, 0.0), axis=1, keepdims=True)
+        mask = row_valid * col_valid
+        values = pair_ref[row]
+        centered = values.astype(jnp.float32) - total(values) * (1.0 / width)
+        square = centered * centered
+        high = square.astype(jnp.bfloat16)
+        low = (square - high.astype(jnp.float32)).astype(jnp.bfloat16)
+        spread = (total(high) + total(low)) * (1.0 / width)
+        normed = (centered * lax.rsqrt(spread + 1e-05)).astype(jnp.bfloat16)
+        normed_ref[pl.ds(row * cols, cols), :] = normed
+        proj = dot_rows(turned, normed)
+        held[row] = sigmoid(proj[:hidden]) * proj[hidden : 2 * hidden] * mask
+        held[rows + row] = sigmoid(proj[2 * hidden : 3 * hidden]) * proj[3 * hidden :] * mask
+    step = 16
+    for first_channel in range(0, hidden, step):
+        part = slice(first_channel, first_channel + step)
+        sent_ref[part] = jnp.transpose(held[:, part, :], (1, 0, 2)).astype(jnp.bfloat16)
+
+
+def project_blocks(pair, token_valid, w_pair):
+    rows, cols, width = pair.shape
+    hidden = w_pair.shape[1] // 4
+    return pl.pallas_call(
+        project_kernel,
+        out_shape=(
+            jax.ShapeDtypeStruct((hidden, 2 * rows, cols), jnp.bfloat16),
+            jax.ShapeDtypeStruct((rows * cols, width), jnp.bfloat16),
+        ),
+        in_specs=[pl.BlockSpec(memory_space=pltpu.VMEM)] * 3,
+        out_specs=(pl.BlockSpec(memory_space=pltpu.VMEM),) * 2,
+        scratch_shapes=[pltpu.VMEM((2 * rows, hidden, cols), jnp.float32)],
+        compiler_params=pltpu.CompilerParams(vmem_limit_bytes=32 * 1024 * 1024),
+    )(pair, token_valid.reshape(1, -1), w_pair)
+
+
+def plane_kernel(got_ref, other_ref, out_ref):
     blocks, rows, cols = out_ref.shape
     chips = blocks // 2
     size = chips * rows
@@ -50,10 +103,11 @@
         other += dot_rows(left, flat(other_ref[part, :, :]))
     own = own.astype(jnp.bfloat16)
     other = other.astype(jnp.bfloat16)
+    core = lax.axis_index("wide") % 2
     source = lax.broadcasted_iota(jnp.int32, (cols, cols), 0)
     target = lax.broadcasted_iota(jnp.int32, (cols, cols), 1)
     seat = source % (cols // 2)
-    seat_core = jnp.where(source < cols // 2, core_ref[0], 1 - core_ref[0])
+    seat_core = jnp.where(source < cols // 2, core, 1 - core)
     place = (seat // rows * 2 + seat_core) * rows + seat % rows
     order = jnp.where(place == target, 1.0, 0.0).astype(jnp.bfloat16)
     for half in range(2):
@@ -65,19 +119,18 @@
         )
 
 
-def plane_blocks(core, got, other):
+def plane_blocks(got, other):
     blocks, rows, cols = other.shape
     return pl.pallas_call(
         plane_kernel,
         out_shape=jax.ShapeDtypeStruct((blocks, rows, cols), jnp.bfloat16),
         in_specs=[
-            pl.BlockSpec(memory_space=pltpu.SMEM),
             pl.BlockSpec(memory_space=pltpu.VMEM),
             pl.BlockSpec(memory_space=pltpu.VMEM),
         ],
         out_specs=pl.BlockSpec(memory_space=pltpu.VMEM),
         compiler_params=pltpu.CompilerParams(vmem_limit_bytes=32 * 1024 * 1024),
-    )(core, got, other)
+    )(got, other)
 
 
 def make(wide, row):
@@ -86,30 +139,12 @@
     def shards(pair, token_valid, w_pair, w_gate, w_out):
         rows_dev, cols_dev, width = pair.shape
         hidden = w_out.shape[0]
-        valid = token_valid.astype(jnp.float32)
-        row_valid = lax.dynamic_slice_in_dim(
-            valid, lax.axis_index("wide") * rows_dev, rows_dev, 0
-        )
-        col_valid = lax.dynamic_slice_in_dim(valid, lax.axis_index("row") * cols_dev, cols_dev, 0)
-        weight_mask = (row_valid[:, None] * col_valid[None, :]).reshape(1, -1)
-        normed = normalize(pair.astype(jnp.float32), 2).astype(jnp.bfloat16)
-        normed = normed.reshape(-1, width)
-        proj = jnp.einsum("de,nd->en", w_pair, normed, preferred_element_type=jnp.float32)
-        left = jax.nn.sigmoid(proj[:hidden]) * proj[hidden : 2 * hidden] * weight_mask
-        right = jax.nn.sigmoid(proj[2 * hidden : 3 * hidden]) * proj[3 * hidden :] * weight_mask
-        sent = jnp.concatenate(
-            [
-                left.astype(jnp.bfloat16).reshape(hidden, rows_dev, cols_dev),
-                right.astype(jnp.bfloat16).reshape(hidden, rows_dev, cols_dev),
-            ],
-            axis=1,
-        )
+        sent, normed = project_blocks(pair, token_valid, w_pair)
         got = exchange(sent, groups)
         other = lax.ppermute(
             got[:, rows_dev:, :], "wide", [(i, i ^ 1) for i in range(wide)]
         )
-        core = (lax.axis_index("wide") % 2).astype(jnp.int32).reshape(1)
-        plane = plane_blocks(core, got, other)
+        plane = plane_blocks(got, other)
         returned = exchange(plane, groups)
         gating = jax.nn.sigmoid(
             jnp.einsum("nd,de->ne", normed, w_gate, preferred_element_type=jnp.float32)

time: 66.9 us -> 65.5 us (0.979)
  other arithmetic: 5.64 us -> 0.54 us
  local copies, waits for them, and re-layouts: 0.72 us -> 3.43 us
  Pallas kernels: 1.2 us -> 2.83 us
    unnamed x8 -> x11, local copies, waits for them, and re-layouts: 0.05 us -> 3.29 us
    convert_element_type x3 -> x0, other arithmetic: 2.32 us -> none  [the longest x1 1.29 us: shards(): normed = normalize(pair.astype(jnp.float32), 2).astype(jnp.bfloat16)]
    pallas_call x0 -> x1, Pallas kernels: none -> 1.64 us  [project_blocks(): pl.pallas_call(project_kernel, out_shape=(jax.ShapeDtypeStruct((hidden, 2...]
    reduce_sum x2 -> x1, other arithmetic: 1.55 us -> 0.22 us  [normalize(): spread = jnp.mean(centered * centered, axis=axis, keepdims=True)]
    reduce_sum x2 -> x1, other arithmetic: 1.26 us -> 0.17 us  [normalize(): mean = jnp.mean(values, axis=axis, keepdims=True)]
where the time goes in v3:
time: 65.5 us; the launch traced here: 64.3 us
  blocking collectives  33.1 us (51%)
  waiting for transfers between devices  12.8 us (20%)
  starting transfers between devices  10.2 us (16%)
  local copies, waits for them, and re-layouts  3.43 us (5%)
  Pallas kernels  2.83 us (4%)
  matrix products  1.25 us (2%)
    all_to_all x1, blocking collectives, exchange(): lax.all_to_all(blocks, ('wide', 'row'), split_axis=0, concat_axis=0, tile...  33.1 us
    all_to_all x1, waiting for transfers between devices, exchange(): lax.all_to_all(blocks, ('wide', 'row'), split_axis=0, concat_axis=0, tile...  11.6 us
    all_to_all x1, starting transfers between devices, exchange(): lax.all_to_all(blocks, ('wide', 'row'), split_axis=0, concat_axis=0, tile...  7.46 us
    unnamed x11, local copies, waits for them, and re-layouts  3.29 us
    ppermute x1, starting transfers between devices, shards(): lax.ppermute(got[:, rows_dev:, :], 'wide', [(i, i ^ 1) for i in range(wid...  2.76 us
    pallas_call x1, Pallas kernels, project_blocks(): pl.pallas_call(project_kernel, out_shape=(jax.ShapeDtypeStruct((hidden, 2...  1.64 us
  transfers between devices with their start and end apart: 2, of which 2 were waited for; matrix products, arithmetic and copies ran while one was open for 0% of the time, Pallas kernels for 0%

profile of v3, /device:TPU:1, one launch (start us, length us, event | category | flops | bytes accessed | tf_op | source)
XLA Modules:
  0.0 64.3 jit_solution(13309704879437132435)
XLA Ops:
  0.0 0.0 copy-start
  0.0 0.0 copy-start.1
  0.0 1.0 %copy-done.1 = bf16[4,256,128]{2,1,0:T(8,128)(2,1)S(1)} copy-done((bf16[4,256,128]{2,1,0:T(8,128)(2,1)S(1)}, bf16[4,256,128]{2,1,0:T(8,128)(2,1)}, u32[]{:S(2)}) %copy-start.1) | copy-done | bytes 262168
  1.0 0.0 copy-start.2
  1.0 0.9 %copy-done.2 = bf16[128,512]{1,0:T(8,128)(2,1)S(1)} copy-done((bf16[128,512]{1,0:T(8,128)(2,1)S(1)}, bf16[128,512]{1,0:T(8,128)(2,1)}, u32[]{:S(2)}) %copy-start.2) | copy-done | bytes 131096
  1.9 0.0 copy-start.3
  1.9 0.7 %copy-done.3 = s32[512]{0:T(512)S(1)} copy-done((s32[512]{0:T(512)S(1)}, s32[512]{0:T(512)}, u32[]{:S(2)}) %copy-start.3) | copy-done | bytes 2072
  2.5 1.6 %shard_map.55 = (bf16[128,8,256]{2,1,0:T(8,128)(2,1)S(1)}, bf16[1024,128]{1,0:T(8,128)(2,1)S(1)}) custom-call(bf16[4,256,128]{2,1,0:T(8,128)(2,1)S(1)} %copy-done.1, s32[1,512]{1,0:T(1,128)S(1)} %bitcast.8, bf16[128,512]{1,0:T(8,128)(2,1)S(1)} %copy-done.2), custom_call_target="tpu_custom_call" | custom-call | tf_op jit(solution)/shard_map/pallas_call | solution.py:76
  4.2 33.1 %all_to_all.10.got_ref = bf16[128,8,256]{2,1,0:T(8,128)(2,1)S(1)} all-to-all(bf16[128,8,256]{2,1,0:T(8,128)(2,1)S(1)} %get-tuple-element.8), channel_id=1, replica_groups={{0,4,8,12,16,20,24,28,32,36,40,44,48,52,56,60,64,68,72,76,80,84,88,92,9..., dimensions={0} | all-to-all | bytes 1048576 | tf_op jit(solution)/shard_map/all_to_all | solution.py:25
  37.3 0.1 slice.4
  37.5 2.8 %collective-permute-start = (bf16[128,4,256]{2,1,0:T(4,128)(2,1)S(1)}, bf16[128,4,256]{2,1,0:T(4,128)(2,1)S(1)}, u32[]{:S(2)}, u32[]{:S(2)}) collective-permute-start(bf16[128,4,256]{2,1,0:T(4,128)(2,1)S(1)} %slice.4), channel_id=1, source_target_pairs={{0,2},{2,0},{4,6},{6,4},{8,10},{10,8},{12,14},{14,12},{16,18},{18,... | collective-permute-start | bytes 786440 | tf_op jit(solution)/shard_map/ppermute | solution.py:144
  40.2 1.2 %collective-permute-done.other_ref = bf16[128,4,256]{2,1,0:T(4,128)(2,1)S(1)} collective-permute-done((bf16[128,4,256]{2,1,0:T(4,128)(2,1)S(1)}, bf16[128,4,256]{2,1,0:T(4,128)(2,1)S(1)}, u32[]{:S(2)}, u32[]{:S(2)}) %collective-permute-start) | collective-permute-done | bytes 262176 | tf_op jit(solution)/shard_map/ppermute | solution.py:144
  41.4 1.2 %shard_map.56 = bf16[128,4,256]{2,1,0:T(4,128)(2,1)} custom-call(bf16[128,8,256]{2,1,0:T(8,128)(2,1)S(1)} %all_to_all.10.got_ref, bf16[128,4,256]{2,1,0:T(4,128)(2,1)S(1)} %collective-permute-done.other_ref), custom_call_target="tpu_custom_call" | custom-call | tf_op jit(solution)/shard_map/pallas_call | solution.py:124
  42.6 7.5 %all-to-all-start.1 = ((bf16[128,4,256]{2,1,0:T(4,128)(2,1)}), bf16[128,4,256]{2,1,0:T(4,128)(2,1)S(1)}, u32[]{:S(2)}, u32[]{:S(2)}) async-start(bf16[128,4,256]{2,1,0:T(4,128)(2,1)} %shard_map.56), calls=%async_computation.1 | async-start | bytes 524288 | tf_op jit(solution)/shard_map/all_to_all | solution.py:25
  50.1 0.0 copy-done
  50.1 0.3 fusion.2
  50.4 11.6 %all-to-all-done.1 = bf16[128,4,256]{2,1,0:T(4,128)(2,1)S(1)} async-done(((bf16[128,4,256]{2,1,0:T(4,128)(2,1)}), bf16[128,4,256]{2,1,0:T(4,128)(2,1)S(1)}, u32[]{:S(2)}, u32[]{:S(2)}) %all-to-all-start.1) | async-done | bytes 262176 | tf_op jit(solution)/shard_map/all_to_all | solution.py:25
  62.0 0.2 convert_reduce_fusion
  62.1 0.2 fusion.6
  62.4 0.1 fusion.7
  62.5 0.0 copy-start.4
  62.6 0.7 %copy-done.4 = bf16[128,128]{1,0:T(8,128)(2,1)S(1)} copy-done((bf16[128,128]{1,0:T(8,128)(2,1)S(1)}, bf16[128,128]{1,0:T(8,128)(2,1)}, u32[]{:S(2)}) %copy-start.4) | copy-done | bytes 32792
  63.3 1.0 %fusion.3 = bf16[1024,128]{1,0:T(8,128)(2,1)} fusion(f32[1024,128]{1,0:T(8,128)S(1)} %fusion.2, bf16[128,1024]{1,0:T(8,128)(2,1)S(1)} %bitcast.10, bf16[128,128]{1,0:T(8,128)(2,1)S(1)} %copy-done.4), kind=kOutput, calls=%fused_computation.5 | convolution fusion | flops 33816576 | bytes 1081344 | tf_op jit(solution)/shard_map/hn,hc->nc/dot_general | solution.py:153
  (3 shorter events, 0.0 us)
Async XLA Ops:
  0.0 50.1 %copy-start = (bf16[128,128]{1,0:T(8,128)(2,1)S(1)}, bf16[128,128]{1,0:T(8,128)(2,1)}, u32[]{:S(2)}) copy-start(bf16[128,128]{1,0:T(8,128)(2,1)} %param.8) | copy-start | bytes 98308
  0.0 1.0 %copy-start.1 = (bf16[4,256,128]{2,1,0:T(8,128)(2,1)S(1)}, bf16[4,256,128]{2,1,0:T(8,128)(2,1)}, u32[]{:S(2)}) copy-start(bf16[4,256,128]{2,1,0:T(8,128)(2,1)} %pair_ref.1) | copy-start | bytes 786436
  1.0 0.9 %copy-start.2 = (bf16[128,512]{1,0:T(8,128)(2,1)S(1)}, bf16[128,512]{1,0:T(8,128)(2,1)}, u32[]{:S(2)}) copy-start(bf16[128,512]{1,0:T(8,128)(2,1)} %w_ref.1) | copy-start | bytes 393220
  1.9 0.7 %copy-start.3 = (s32[512]{0:T(512)S(1)}, s32[512]{0:T(512)}, u32[]{:S(2)}) copy-start(s32[512]{0:T(512)} %param.6) | copy-start | bytes 6148
  37.5 3.9 %collective-permute-start = (bf16[128,4,256]{2,1,0:T(4,128)(2,1)S(1)}, bf16[128,4,256]{2,1,0:T(4,128)(2,1)S(1)}, u32[]{:S(2)}, u32[]{:S(2)}) collective-permute-start(bf16[128,4,256]{2,1,0:T(4,128)(2,1)S(1)} %slice.4), channel_id=1, source_target_pairs={{0,2},{2,0},{4,6},{6,4},{8,10},{10,8},{12,14},{14,12},{16,18},{18,... | collective-permute-start | bytes 786440 | tf_op jit(solution)/shard_map/ppermute | solution.py:144
  42.6 19.4 %all-to-all-start.1 = ((bf16[128,4,256]{2,1,0:T(4,128)(2,1)}), bf16[128,4,256]{2,1,0:T(4,128)(2,1)S(1)}, u32[]{:S(2)}, u32[]{:S(2)}) async-start(bf16[128,4,256]{2,1,0:T(4,128)(2,1)} %shard_map.56), calls=%async_computation.1 | async-start | bytes 524288 | tf_op jit(solution)/shard_map/all_to_all | solution.py:25
  62.5 0.8 %copy-start.4 = (bf16[128,128]{1,0:T(8,128)(2,1)S(1)}, bf16[128,128]{1,0:T(8,128)(2,1)}, u32[]{:S(2)}) copy-start(bf16[128,128]{1,0:T(8,128)(2,1)} %param.9) | copy-start | bytes 98308

commit v4 on v3

v4 whole, which is shorter than its diff:
```python
import jax
import jax.numpy as jnp
from jax import lax
from jax.experimental import pallas as pl
from jax.experimental.pallas import tpu as pltpu
from jax.sharding import PartitionSpec as P

VMEM = pl.BlockSpec(memory_space=pltpu.VMEM)
ANY = pl.BlockSpec(memory_space=pl.ANY)


def chip_groups(wide, row):
    chips = wide // 2
    return [
        [(chip * 2 + core) * row + half for half in range(row) for chip in range(chips)]
        for core in range(2)
    ]


def exchange(blocks, groups):
    return lax.all_to_all(
        blocks, ("wide", "row"), split_axis=0, concat_axis=0, tiled=True, axis_index_groups=groups
    )


def dot_rows(left, right):
    return lax.dot_general(
        left, right, (((1,), (1,)), ((), ())), preferred_element_type=jnp.float32
    )


def sigmoid(values):
    return 0.5 * jnp.tanh(0.5 * values) + 0.5


def project_kernel(
    pair_hbm, valid_hbm, w_hbm, gate_hbm, out_hbm,
    sent_ref, normed_ref, gate_ref, out_ref,
    pair_ref, valid_ref, w_ref, held, arrived,
):
    rows, cols, width = pair_ref.shape
    hidden = sent_ref.shape[0]
    pieces = [(w_hbm, w_ref)]
    pieces += [(pair_hbm.at[row], pair_ref.at[row]) for row in range(rows)]
    pieces += [(valid_hbm, valid_ref), (gate_hbm, gate_ref), (out_hbm, out_ref)]
    copies = [
        pltpu.make_async_copy(source, target, arrived.at[index])
        for index, (source, target) in enumerate(pieces)
    ]
    for copy in copies:
        copy.start()
    ones = jnp.ones((width, width), jnp.bfloat16)

    def total(values):
        return jnp.dot(values, ones, preferred_element_type=jnp.float32)

    copies[0].wait()
    turned = w_ref[...].T
    copies[rows + 1].wait()
    valid = valid_ref[...].astype(jnp.float32)
    seat = lax.broadcasted_iota(jnp.int32, valid.shape, 1)
    first = lax.axis_index("wide") * rows
    col_valid = jnp.where(lax.axis_index("row") == 0, valid[:, :cols], valid[:, cols:])
    for row in range(rows):
        row_valid = jnp.sum(jnp.where(seat == first + row, valid, 0.0), axis=1, keepdims=True)
        mask = row_valid * col_valid
        copies[1 + row].wait()
        values = pair_ref[row]
        centered = values.astype(jnp.float32) - total(values) * (1.0 / width)
        square = centered * centered
        high = square.astype(jnp.bfloat16)
        low = (square - high.astype(jnp.float32)).astype(jnp.bfloat16)
        spread = (total(high) + total(low)) * (1.0 / width)
        normed = (centered * lax.rsqrt(spread + 1e-05)).astype(jnp.bfloat16)
        normed_ref[pl.ds(row * cols, cols), :] = normed
        proj = dot_rows(turned, normed)
        held[row] = sigmoid(proj[:hidden]) * proj[hidden : 2 * hidden] * mask
        held[rows + row] = sigmoid(proj[2 * hidden : 3 * hidden]) * proj[3 * hidden :] * mask
    step = 16
    for first_channel in range(0, hidden, step):
        part = slice(first_channel, first_channel + step)
        sent_ref[part] = jnp.transpose(held[:, part, :], (1, 0, 2)).astype(jnp.bfloat16)
    copies[rows + 2].wait()
    copies[rows + 3].wait()


def project_blocks(pair, token_valid, w_pair, w_gate, w_out):
    rows, cols, width = pair.shape
    hidden = w_out.shape[0]
    valid = token_valid.reshape(1, -1)
    return pl.pallas_call(
        project_kernel,
        out_shape=(
            jax.ShapeDtypeStruct((hidden, 2 * rows, cols), jnp.bfloat16),
            jax.ShapeDtypeStruct((rows * cols, width), jnp.bfloat16),
            jax.ShapeDtypeStruct(w_gate.shape, jnp.bfloat16),
            jax.ShapeDtypeStruct(w_out.shape, jnp.bfloat16),
        ),
        in_specs=[ANY] * 5,
        out_specs=(VMEM,) * 4,
        scratch_shapes=[
            pltpu.VMEM(pair.shape, jnp.bfloat16),
            pltpu.VMEM(valid.shape, jnp.int32),
            pltpu.VMEM(w_pair.shape, jnp.bfloat16),
            pltpu.VMEM((2 * rows, hidden, cols), jnp.float32),
            pltpu.SemaphoreType.DMA((rows + 4,)),
        ],
    )(pair, valid, w_pair, w_gate, w_out)


def flat(values):
    chips, rows, cols = values.shape
    return values.astype(jnp.float32).reshape(chips * rows, cols).astype(jnp.bfloat16)


def column_order(core, rows, cols):
    source = lax.broadcasted_iota(jnp.int32, (cols // 2, cols), 0)
    target = lax.broadcasted_iota(jnp.int32, (cols // 2, cols), 1)
    place = (source // rows * 2 + core) * rows + source % rows
    return jnp.where(place == target, 1.0, 0.0).astype(jnp.bfloat16)


def own_kernel(got_ref, normed_ref, gate_ref, left_ref, own_ref, gating_ref):
    blocks, both, cols = got_ref.shape
    rows, chips = both // 2, blocks // 2
    size = chips * rows
    own = jnp.zeros((size, size), jnp.float32)
    for half in range(2):
        part = pl.ds(half * chips, chips)
        left = flat(got_ref[part, :rows, :])
        left_ref[half] = left
        own += dot_rows(left, flat(got_ref[part, rows:, :]))
    own = own.astype(jnp.bfloat16)
    order = column_order(lax.axis_index("wide") % 2, rows, cols)
    for half in range(2):
        span = slice(half * (size // 2), (half + 1) * (size // 2))
        own_ref[half] = jnp.dot(own[:, span], order, preferred_element_type=jnp.float32)
    gating_ref[...] = sigmoid(
        jnp.dot(normed_ref[...], gate_ref[...], preferred_element_type=jnp.float32)
    )


def own_part(got, normed, w_gate):
    blocks, both, cols = got.shape
    size = blocks // 2 * (both // 2)
    return pl.pallas_call(
        own_kernel,
        out_shape=(
            jax.ShapeDtypeStruct((2, size, cols), jnp.bfloat16),
            jax.ShapeDtypeStruct((2, size, cols), jnp.float32),
            jax.ShapeDtypeStruct(normed.shape, jnp.float32),
        ),
        in_specs=[VMEM] * 3,
        out_specs=(VMEM,) * 3,
        cost_estimate=pl.CostEstimate(
            flops=4 * size * size * cols, bytes_accessed=3 * 1024 * 1024, transcendentals=0
        ),
    )(got, normed, w_gate)


def plane_kernel(other_ref, left_ref, own_ref, out_ref):
    blocks, rows, cols = out_ref.shape
    chips = blocks // 2
    size = chips * rows
    other = jnp.zeros((size, size), jnp.float32)
    for half in range(2):
        other += dot_rows(left_ref[half], flat(other_ref[pl.ds(half * chips, chips)]))
    other = other.astype(jnp.bfloat16)
    order = column_order(1 - lax.axis_index("wide") % 2, rows, cols)
    for half in range(2):
        span = slice(half * (size // 2), (half + 1) * (size // 2))
        placed = own_ref[half] + jnp.dot(
            other[:, span], order, preferred_element_type=jnp.float32
        )
        out_ref[pl.ds(half * chips, chips)] = placed.reshape(chips, rows, cols).astype(
            jnp.bfloat16
        )


def plane_blocks(other, left, own):
    return pl.pallas_call(
        plane_kernel,
        out_shape=jax.ShapeDtypeStruct(other.shape, jnp.bfloat16),
        in_specs=[VMEM] * 3,
        out_specs=VMEM,
    )(other, left, own)


def finish_kernel(returned_ref, gating_ref, out_ref, update_hbm, staged, left_device):
    rows, cols, width = staged.shape
    hidden = returned_ref.shape[0]
    turned = jnp.transpose(returned_ref[...].astype(jnp.float32), (1, 0, 2))
    copies = []
    for row in range(rows):
        values = turned[row]
        mean = jnp.sum(values, axis=0, keepdims=True) * (1.0 / hidden)
        centered = values - mean
        spread = jnp.sum(centered * centered, axis=0, keepdims=True) * (1.0 / hidden)
        tri_norm = (centered * lax.rsqrt(spread + 1e-05)).astype(jnp.bfloat16)
        mixed = lax.dot_general(
            tri_norm, out_ref[...], (((0,), (0,)), ((), ())), preferred_element_type=jnp.float32
        )
        staged[row] = (gating_ref[pl.ds(row * cols, cols), :] * mixed).astype(jnp.bfloat16)
        copy = pltpu.make_async_copy(staged.at[row], update_hbm.at[row], left_device.at[row])
        copy.start()
        copies.append(copy)
    for copy in copies:
        copy.wait()


def finish(returned, gating, w_out, shape):
    return pl.pallas_call(
        finish_kernel,
        out_shape=jax.ShapeDtypeStruct(shape, jnp.bfloat16),
        in_specs=[VMEM] * 3,
        out_specs=ANY,
        scratch_shapes=[
            pltpu.VMEM(shape, jnp.bfloat16),
            pltpu.SemaphoreType.DMA((shape[0],)),
        ],
    )(returned, gating, w_out)


def make(wide, row):
    groups = chip_groups(wide, row)

    def shards(pair, token_valid, w_pair, w_gate, w_out):
        rows = pair.shape[0]
        sent, normed, w_gate, w_out = project_blocks(pair, token_valid, w_pair, w_gate, w_out)
        got = exchange(sent, groups)
        other = lax.ppermute(got[:, rows:, :], "wide", [(i, i ^ 1) for i in range(wide)])
        left, own, gating = own_part(got, normed, w_gate)
        returned = exchange(plane_blocks(other, left, own), groups)
        return finish(returned, gating, w_out, pair.shape)

    return shards


def solution(mesh):
    placed = (P("wide", "row", None), P(), P(), P(), P())
    return jax.shard_map(
        make(mesh.shape["wide"], mesh.shape["row"]),
        mesh=mesh,
        in_specs=placed,
        out_specs=P("wide", "row", None),
        check_vma=False,
    )
```

time: 65.5 us -> 69.6 us (1.063)
  the two profiles are of different devices: /device:TPU:1 before, /device:TPU:32 now
where the time goes in v4:
time: 69.6 us; the launch traced here: 69.3 us
  blocking collectives  55.9 us (80%)
  Pallas kernels  11.9 us (17%)
  local copies, waits for them, and re-layouts  1.41 us (2%)
    all_to_all x2, blocking collectives, exchange(): lax.all_to_all(blocks, ('wide', 'row'), split_axis=0, concat_axis=0, tile...  55.9 us
    pallas_call x1, Pallas kernels, project_blocks(): pl.pallas_call(project_kernel, out_shape=(jax.ShapeDtypeStruct((hidden, 2...  4.51 us
    pallas_call x1, Pallas kernels, own_part(): pl.pallas_call(own_kernel, out_shape=(jax.ShapeDtypeStruct((2, size, cols...  2.62 us
    pallas_call x1, Pallas kernels, plane_blocks(): pl.pallas_call(plane_kernel, out_shape=jax.ShapeDtypeStruct(other.shape,...  2.41 us
    pallas_call x1, Pallas kernels, finish(): pl.pallas_call(finish_kernel, out_shape=jax.ShapeDtypeStruct(shape, jnp.b...  2.34 us
  transfers between devices with their start and end apart: 1, of which 0 were waited for; matrix products, arithmetic and copies ran while one was open for 0% of the time, Pallas kernels for 4%

profile of v4, /device:TPU:32, one launch (start us, length us, event | category | flops | bytes accessed | tf_op | source)
XLA Modules:
  0.0 69.3 jit_solution(16441660776102068276)
XLA Ops:
  0.0 4.5 %shard_map.55 = (bf16[128,8,256]{2,1,0:T(8,128)(2,1)}, bf16[1024,128]{1,0:T(8,128)(2,1)}, bf16[128,128]{1,0:T(8,128)(2,1)}, bf16[128,128]{1,0:T(8,128)(2,1)}) custom-call(bf16[4,256,128]{2,1,0:T(8,128)(2,1)} %pair_hbm.1, s32[1,512]{1,0:T(1,128)} %bitcast.1, bf16[128,512]{1,0:T(8,128)(2,1)} %w_hbm.1, bf16[128,128]{1,0:T(8,128)(2,1)} %gate_hbm.1, ...), custom_call_target="tpu_custom_call" | custom-call | tf_op jit(solution)/shard_map/pallas_call | solution.py:91
  4.5 34.2 %all_to_all.10.got_ref = bf16[128,8,256]{2,1,0:T(8,128)(2,1)S(1)} all-to-all(bf16[128,8,256]{2,1,0:T(8,128)(2,1)} %get-tuple-element.12), channel_id=1, replica_groups={{0,4,8,12,16,20,24,28,32,36,40,44,48,52,56,60,64,68,72,76,80,84,88,92,9..., dimensions={0} | all-to-all | bytes 1048576 | tf_op jit(solution)/shard_map/all_to_all | solution.py:21
  38.7 0.0 copy-start
  38.7 0.1 slice.4
  38.8 0.1 collective-permute-start
  38.9 0.6 copy-done
  39.5 2.6 %shard_map.56 = (bf16[2,256,256]{2,1,0:T(8,128)(2,1)}, f32[2,256,256]{2,1,0:T(8,128)}, f32[1024,128]{1,0:T(8,128)}) custom-call(bf16[128,8,256]{2,1,0:T(8,128)(2,1)} %copy-done, bf16[1024,128]{1,0:T(8,128)(2,1)} %get-tuple-element.13.normed_ref, bf16[128,128]{1,0:T(8,128)(2,1)} %get-tuple-element.14.gate_ref), custom_call_target="tpu_custom_call" | custom-call | flops 67108864 | bytes 3145728 | tf_op jit(solution)/shard_map/pallas_call | solution.py:146
  42.1 0.0 collective-permute-done.other_ref
  42.1 0.0 copy-start.1
  42.1 0.7 %copy-done.1 = bf16[128,4,256]{2,1,0:T(4,128)(2,1)} copy-done((bf16[128,4,256]{2,1,0:T(4,128)(2,1)}, bf16[128,4,256]{2,1,0:T(4,128)(2,1)S(1)}, u32[]{:S(2)}) %copy-start.1) | copy-done | bytes 262168
  42.8 2.4 %shard_map.57 = bf16[128,4,256]{2,1,0:T(4,128)(2,1)} custom-call(bf16[128,4,256]{2,1,0:T(4,128)(2,1)} %copy-done.1, bf16[2,256,256]{2,1,0:T(8,128)(2,1)} %get-tuple-element.15.left_ref, f32[2,256,256]{2,1,0:T(8,128)} %get-tuple-element.16.own_ref), custom_call_target="tpu_custom_call" | custom-call | tf_op jit(solution)/shard_map/pallas_call | solution.py:181
  45.2 21.7 %all_to_all.11.returned_ref = bf16[128,4,256]{2,1,0:T(4,128)(2,1)} all-to-all(bf16[128,4,256]{2,1,0:T(4,128)(2,1)} %shard_map.57), channel_id=1, replica_groups={{0,4,8,12,16,20,24,28,32,36,40,44,48,52,56,60,64,68,72,76,80,84,88,92,9..., dimensions={0} | all-to-all | bytes 524288 | tf_op jit(solution)/shard_map/all_to_all | solution.py:21
  66.9 2.3 %shard_map.58 = bf16[4,256,128]{2,1,0:T(8,128)(2,1)} custom-call(bf16[128,4,256]{2,1,0:T(4,128)(2,1)} %all_to_all.11.returned_ref, f32[1024,128]{1,0:T(8,128)} %get-tuple-element.17.gating_ref, bf16[128,128]{1,0:T(8,128)(2,1)} %get-tuple-element.18.out_ref), custom_call_target="tpu_custom_call" | custom-call | tf_op jit(solution)/shard_map/pallas_call | solution.py:212
Async XLA Ops:
  38.7 0.8 %copy-start = (bf16[128,8,256]{2,1,0:T(8,128)(2,1)}, bf16[128,8,256]{2,1,0:T(8,128)(2,1)S(1)}, u32[]{:S(2)}) copy-start(bf16[128,8,256]{2,1,0:T(8,128)(2,1)S(1)} %all_to_all.10.got_ref) | copy-start | bytes 1572868
  38.8 3.3 %collective-permute-start = (bf16[128,4,256]{2,1,0:T(4,128)(2,1)S(1)}, bf16[128,4,256]{2,1,0:T(4,128)(2,1)S(1)}, u32[]{:S(2)}, u32[]{:S(2)}) collective-permute-start(bf16[128,4,256]{2,1,0:T(4,128)(2,1)S(1)} %slice.4), channel_id=1, source_target_pairs={{0,2},{2,0},{4,6},{6,4},{8,10},{10,8},{12,14},{14,12},{16,18},{18,... | collective-permute-start | bytes 786440 | tf_op jit(solution)/shard_map/ppermute | solution.py:231
  42.1 0.7 %copy-start.1 = (bf16[128,4,256]{2,1,0:T(4,128)(2,1)}, bf16[128,4,256]{2,1,0:T(4,128)(2,1)S(1)}, u32[]{:S(2)}) copy-start(bf16[128,4,256]{2,1,0:T(4,128)(2,1)S(1)} %collective-permute-done.other_ref) | copy-start | bytes 786436

commit v5 on v4

--- a/solution.py
+++ b/solution.py
@@ -7,6 +7,7 @@
 
 VMEM = pl.BlockSpec(memory_space=pltpu.VMEM)
 ANY = pl.BlockSpec(memory_space=pl.ANY)
+ROOM = pltpu.CompilerParams(vmem_limit_bytes=32 * 1024 * 1024)
 
 
 def chip_groups(wide, row):
@@ -33,30 +34,43 @@
     return 0.5 * jnp.tanh(0.5 * values) + 0.5
 
 
-def project_kernel(
-    pair_hbm, valid_hbm, w_hbm, gate_hbm, out_hbm,
-    sent_ref, normed_ref, gate_ref, out_ref,
-    pair_ref, valid_ref, w_ref, held, arrived,
-):
+def normed_kernel(pair_ref, normed_ref):
     rows, cols, width = pair_ref.shape
-    hidden = sent_ref.shape[0]
-    pieces = [(w_hbm, w_ref)]
-    pieces += [(pair_hbm.at[row], pair_ref.at[row]) for row in range(rows)]
-    pieces += [(valid_hbm, valid_ref), (gate_hbm, gate_ref), (out_hbm, out_ref)]
-    copies = [
-        pltpu.make_async_copy(source, target, arrived.at[index])
-        for index, (source, target) in enumerate(pieces)
-    ]
-    for copy in copies:
-        copy.start()
     ones = jnp.ones((width, width), jnp.bfloat16)
 
     def total(values):
         return jnp.dot(values, ones, preferred_element_type=jnp.float32)
 
-    copies[0].wait()
+    for row in range(rows):
+        values = pair_ref[row]
+        centered = values.astype(jnp.float32) - total(values) * (1.0 / width)
+        square = centered * centered
+        high = square.astype(jnp.bfloat16)
+        low = (square - high.astype(jnp.float32)).astype(jnp.bfloat16)
+        spread = (total(high) + total(low)) * (1.0 / width)
+        normed_ref[pl.ds(row * cols, cols), :] = (
+            centered * lax.rsqrt(spread + 1e-05)
+        ).astype(jnp.bfloat16)
+
+
+def norm_pair(pair):
+    rows, cols, width = pair.shape
+    return pl.pallas_call(
+        normed_kernel,
+        out_shape=jax.ShapeDtypeStruct((rows * cols, width), jnp.bfloat16),
+        in_specs=[VMEM],
+        out_specs=VMEM,
+        compiler_params=ROOM,
+        cost_estimate=pl.CostEstimate(
+            flops=8 * rows * cols * width * width, bytes_accessed=4 * 1024 * 1024, transcendentals=0
+        ),
+    )(pair)
+
+
+def project_kernel(normed_ref, valid_ref, w_ref, sent_ref, held):
+    hidden, both, cols = sent_ref.shape
+    rows = both // 2
     turned = w_ref[...].T
-    copies[rows + 1].wait()
     valid = valid_ref[...].astype(jnp.float32)
     seat = lax.broadcasted_iota(jnp.int32, valid.shape, 1)
     first = lax.axis_index("wide") * rows
@@ -64,48 +78,25 @@
     for row in range(rows):
         row_valid = jnp.sum(jnp.where(seat == first + row, valid, 0.0), axis=1, keepdims=True)
         mask = row_valid * col_valid
-        copies[1 + row].wait()
-        values = pair_ref[row]
-        centered = values.astype(jnp.float32) - total(values) * (1.0 / width)
-        square = centered * centered
-        high = square.astype(jnp.bfloat16)
-        low = (square - high.astype(jnp.float32)).astype(jnp.bfloat16)
-        spread = (total(high) + total(low)) * (1.0 / width)
-        normed = (centered * lax.rsqrt(spread + 1e-05)).astype(jnp.bfloat16)
-        normed_ref[pl.ds(row * cols, cols), :] = normed
-        proj = dot_rows(turned, normed)
+        proj = dot_rows(turned, normed_ref[pl.ds(row * cols, cols), :])
         held[row] = sigmoid(proj[:hidden]) * proj[hidden : 2 * hidden] * mask
         held[rows + row] = sigmoid(proj[2 * hidden : 3 * hidden]) * proj[3 * hidden :] * mask
     step = 16
     for first_channel in range(0, hidden, step):
         part = slice(first_channel, first_channel + step)
         sent_ref[part] = jnp.transpose(held[:, part, :], (1, 0, 2)).astype(jnp.bfloat16)
-    copies[rows + 2].wait()
-    copies[rows + 3].wait()
-
-
-def project_blocks(pair, token_valid, w_pair, w_gate, w_out):
-    rows, cols, width = pair.shape
-    hidden = w_out.shape[0]
-    valid = token_valid.reshape(1, -1)
+
+
+def project_blocks(normed, token_valid, w_pair, rows, hidden):
+    cols = normed.shape[0] // rows
     return pl.pallas_call(
         project_kernel,
-        out_shape=(
-            jax.ShapeDtypeStruct((hidden, 2 * rows, cols), jnp.bfloat16),
-            jax.ShapeDtypeStruct((rows * cols, width), jnp.bfloat16),
-            jax.ShapeDtypeStruct(w_gate.shape, jnp.bfloat16),
-            jax.ShapeDtypeStruct(w_out.shape, jnp.bfloat16),
-        ),
-        in_specs=[ANY] * 5,
-        out_specs=(VMEM,) * 4,
-        scratch_shapes=[
-            pltpu.VMEM(pair.shape, jnp.bfloat16),
-            pltpu.VMEM(valid.shape, jnp.int32),
-            pltpu.VMEM(w_pair.shape, jnp.bfloat16),
-            pltpu.VMEM((2 * rows, hidden, cols), jnp.float32),
-            pltpu.SemaphoreType.DMA((rows + 4,)),
-        ],
-    )(pair, valid, w_pair, w_gate, w_out)
+        out_shape=jax.ShapeDtypeStruct((hidden, 2 * rows, cols), jnp.bfloat16),
+        in_specs=[VMEM] * 3,
+        out_specs=VMEM,
+        scratch_shapes=[pltpu.VMEM((2 * rows, hidden, cols), jnp.float32)],
+        compiler_params=ROOM,
+    )(normed, token_valid.reshape(1, -1), w_pair)
 
 
 def flat(values):
@@ -120,7 +111,10 @@
     return jnp.where(place == target, 1.0, 0.0).astype(jnp.bfloat16)
 
 
-def own_kernel(got_ref, normed_ref, gate_ref, left_ref, own_ref, gating_ref):
+def own_kernel(
+    got_ref, normed_ref, gate_ref, w_out_ref, left_ref, own_ref, gating_ref, held_out_ref
+):
+    held_out_ref[...] = w_out_ref[...]
     blocks, both, cols = got_ref.shape
     rows, chips = both // 2, blocks // 2
     size = chips * rows
@@ -140,7 +134,7 @@
     )
 
 
-def own_part(got, normed, w_gate):
+def own_part(got, normed, w_gate, w_out):
     blocks, both, cols = got.shape
     size = blocks // 2 * (both // 2)
     return pl.pallas_call(
@@ -149,13 +143,15 @@
             jax.ShapeDtypeStruct((2, size, cols), jnp.bfloat16),
             jax.ShapeDtypeStruct((2, size, cols), jnp.float32),
             jax.ShapeDtypeStruct(normed.shape, jnp.float32),
+            jax.ShapeDtypeStruct(w_out.shape, jnp.bfloat16),
         ),
-        in_specs=[VMEM] * 3,
-        out_specs=(VMEM,) * 3,
+        in_specs=[VMEM] * 4,
+        out_specs=(VMEM,) * 4,
+        compiler_params=ROOM,
         cost_estimate=pl.CostEstimate(
             flops=4 * size * size * cols, bytes_accessed=3 * 1024 * 1024, transcendentals=0
         ),
-    )(got, normed, w_gate)
+    )(got, normed, w_gate, w_out)
 
 
 def plane_kernel(other_ref, left_ref, own_ref, out_ref):
@@ -183,6 +179,7 @@
         out_shape=jax.ShapeDtypeStruct(other.shape, jnp.bfloat16),
         in_specs=[VMEM] * 3,
         out_specs=VMEM,
+        compiler_params=ROOM,
     )(other, left, own)
 
 
@@ -218,6 +215,7 @@
             pltpu.VMEM(shape, jnp.bfloat16),
             pltpu.SemaphoreType.DMA((shape[0],)),
         ],
+        compiler_params=ROOM,
     )(returned, gating, w_out)
 
 
@@ -226,10 +224,11 @@
 
     def shards(pair, token_valid, w_pair, w_gate, w_out):
         rows = pair.shape[0]
-        sent, normed, w_gate, w_out = project_blocks(pair, token_valid, w_pair, w_gate, w_out)
+        normed = norm_pair(pair)
+        sent = project_blocks(normed, token_valid, w_pair, rows, w_out.shape[0])
         got = exchange(sent, groups)
         other = lax.ppermute(got[:, rows:, :], "wide", [(i, i ^ 1) for i in range(wide)])
-        left, own, gating = own_part(got, normed, w_gate)
+        left, own, gating, w_out = own_part(got, normed, w_gate, w_out)
         returned = exchange(plane_blocks(other, left, own), groups)
         return finish(returned, gating, w_out, pair.shape)
 

time: 69.6 us -> 61.8 us (0.89)
  the two profiles are of different devices: /device:TPU:32 before, /device:TPU:1 now
where the time goes in v5:
time: 61.8 us; the launch traced here: 60.6 us
  blocking collectives  52.3 us (85%)
  Pallas kernels  3.64 us (6%)
  starting transfers between devices  2.76 us (4%)
  local copies, waits for them, and re-layouts  1.39 us (2%)
    all_to_all x2, blocking collectives, exchange(): lax.all_to_all(blocks, ('wide', 'row'), split_axis=0, concat_axis=0, tile...  52.3 us
    ppermute x1, starting transfers between devices, shards(): lax.ppermute(got[:, rows:, :], 'wide', [(i, i ^ 1) for i in range(wide)])  2.76 us
    unnamed x10, local copies, waits for them, and re-layouts  1.25 us
    pallas_call x1, Pallas kernels, finish(): pl.pallas_call(finish_kernel, out_shape=jax.ShapeDtypeStruct(shape, jnp.b...  1.24 us
  transfers between devices with their start and end apart: 1, of which 1 were waited for; matrix products, arithmetic and copies ran while one was open for 0% of the time, Pallas kernels for 1%

profile of v5, /device:TPU:1, one launch (start us, length us, event | category | flops | bytes accessed | tf_op | source)
XLA Modules:
  0.0 60.6 jit_solution(2630535624349815237)
XLA Ops:
  0.0 0.0 copy-start
  0.0 0.9 %copy-done = bf16[4,256,128]{2,1,0:T(8,128)(2,1)S(1)} copy-done((bf16[4,256,128]{2,1,0:T(8,128)(2,1)S(1)}, bf16[4,256,128]{2,1,0:T(8,128)(2,1)}, u32[]{:S(2)}) %copy-start) | copy-done | bytes 262168
  1.0 0.0 copy-start.1
  1.0 0.0 copy-start.4
  1.0 0.6 shard_map.55.normed_ref
  1.6 0.3 copy-done.1
  1.9 0.0 copy-done.4
  1.9 0.6 %shard_map.56 = bf16[128,8,256]{2,1,0:T(8,128)(2,1)S(1)} custom-call(bf16[1024,128]{1,0:T(8,128)(2,1)S(1)} %shard_map.55.normed_ref, s32[1,512]{1,0:T(1,128)S(1)} %bitcast.1, bf16[128,512]{1,0:T(8,128)(2,1)S(1)} %copy-done.1), custom_call_target="tpu_custom_call" | custom-call | tf_op jit(solution)/shard_map/pallas_call | solution.py:92
  2.5 33.1 %all_to_all.10.got_ref = bf16[128,8,256]{2,1,0:T(8,128)(2,1)S(1)} all-to-all(bf16[128,8,256]{2,1,0:T(8,128)(2,1)S(1)} %shard_map.56), channel_id=1, replica_groups={{0,4,8,12,16,20,24,28,32,36,40,44,48,52,56,60,64,68,72,76,80,84,88,92,9..., dimensions={0} | all-to-all | bytes 1048576 | tf_op jit(solution)/shard_map/all_to_all | solution.py:22
  35.6 0.0 copy-start.2
  35.7 0.0 copy-start.3
  35.7 0.1 slice.4
  35.8 2.8 %collective-permute-start = (bf16[128,4,256]{2,1,0:T(4,128)(2,1)S(1)}, bf16[128,4,256]{2,1,0:T(4,128)(2,1)S(1)}, u32[]{:S(2)}, u32[]{:S(2)}) collective-permute-start(bf16[128,4,256]{2,1,0:T(4,128)(2,1)S(1)} %slice.4), channel_id=1, source_target_pairs={{0,2},{2,0},{4,6},{6,4},{8,10},{10,8},{12,14},{14,12},{16,18},{18,... | collective-permute-start | bytes 786440 | tf_op jit(solution)/shard_map/ppermute | solution.py:230
  38.6 0.0 copy-done.2
  38.6 0.0 copy-done.3
  38.6 0.7 %shard_map.57 = (bf16[2,256,256]{2,1,0:T(8,128)(2,1)S(1)}, f32[2,256,256]{2,1,0:T(8,128)S(1)}, f32[1024,128]{1,0:T(8,128)S(1)}, bf16[128,128]{1,0:T(8,128)(2,1)S(1)}) custom-call(bf16[128,8,256]{2,1,0:T(8,128)(2,1)S(1)} %all_to_all.10.got_ref, bf16[1024,128]{1,0:T(8,128)(2,1)S(1)} %shard_map.55.normed_ref, bf16[128,128]{1,0:T(8,128)(2,1)S(1)} %copy-done.2, ...), custom_call_target="tpu_custom_call" | custom-call | flops 67108864 | bytes 3145728 | tf_op jit(solution)/shard_map/pallas_call | solution.py:140
  39.2 0.5 collective-permute-done.other_ref
  39.7 0.5 shard_map.58
  40.2 19.2 %all_to_all.11.returned_ref = bf16[128,4,256]{2,1,0:T(4,128)(2,1)S(1)} all-to-all(bf16[128,4,256]{2,1,0:T(4,128)(2,1)S(1)} %shard_map.58), channel_id=1, replica_groups={{0,4,8,12,16,20,24,28,32,36,40,44,48,52,56,60,64,68,72,76,80,84,88,92,9..., dimensions={0} | all-to-all | bytes 524288 | tf_op jit(solution)/shard_map/all_to_all | solution.py:22
  59.4 1.2 %shard_map.59 = bf16[4,256,128]{2,1,0:T(8,128)(2,1)} custom-call(bf16[128,4,256]{2,1,0:T(4,128)(2,1)S(1)} %all_to_all.11.returned_ref, f32[1024,128]{1,0:T(8,128)S(1)} %get-tuple-element.11.gating_ref, bf16[128,128]{1,0:T(8,128)(2,1)S(1)} %get-tuple-element.12.out_ref), custom_call_target="tpu_custom_call" | custom-call | tf_op jit(solution)/shard_map/pallas_call | solution.py:209
Async XLA Ops:
  0.0 0.9 %copy-start = (bf16[4,256,128]{2,1,0:T(8,128)(2,1)S(1)}, bf16[4,256,128]{2,1,0:T(8,128)(2,1)}, u32[]{:S(2)}) copy-start(bf16[4,256,128]{2,1,0:T(8,128)(2,1)} %pair_ref.1) | copy-start | bytes 786436
  1.0 0.9 %copy-start.1 = (bf16[128,512]{1,0:T(8,128)(2,1)S(1)}, bf16[128,512]{1,0:T(8,128)(2,1)}, u32[]{:S(2)}) copy-start(bf16[128,512]{1,0:T(8,128)(2,1)} %w_ref.1) | copy-start | bytes 393220
  1.0 0.9 %copy-start.4 = (s32[512]{0:T(512)S(1)}, s32[512]{0:T(512)}, u32[]{:S(2)}) copy-start(s32[512]{0:T(512)} %param.6) | copy-start | bytes 6148
  35.6 2.9 %copy-start.2 = (bf16[128,128]{1,0:T(8,128)(2,1)S(1)}, bf16[128,128]{1,0:T(8,128)(2,1)}, u32[]{:S(2)}) copy-start(bf16[128,128]{1,0:T(8,128)(2,1)} %gate_ref.1) | copy-start | bytes 98308
  35.7 2.9 %copy-start.3 = (bf16[128,128]{1,0:T(8,128)(2,1)S(1)}, bf16[128,128]{1,0:T(8,128)(2,1)}, u32[]{:S(2)}) copy-start(bf16[128,128]{1,0:T(8,128)(2,1)} %w_out_ref.1) | copy-start | bytes 98308
  35.8 3.9 %collective-permute-start = (bf16[128,4,256]{2,1,0:T(4,128)(2,1)S(1)}, bf16[128,4,256]{2,1,0:T(4,128)(2,1)S(1)}, u32[]{:S(2)}, u32[]{:S(2)}) collective-permute-start(bf16[128,4,256]{2,1,0:T(4,128)(2,1)S(1)} %slice.4), channel_id=1, source_target_pairs={{0,2},{2,0},{4,6},{6,4},{8,10},{10,8},{12,14},{14,12},{16,18},{18,... | collective-permute-start | bytes 786440 | tf_op jit(solution)/shard_map/ppermute | solution.py:230

commit v6 on v5

--- a/solution.py
+++ b/solution.py
@@ -1,3 +1,5 @@
+import functools
+
 import jax
 import jax.numpy as jnp
 from jax import lax
@@ -10,10 +12,28 @@
 ROOM = pltpu.CompilerParams(vmem_limit_bytes=32 * 1024 * 1024)
 
 
-def chip_groups(wide, row):
-    chips = wide // 2
+Y, Z, X = 4, 8, 4
+LEAD = (2, 5, 2)
+
+
+def group_order(chips, row):
+    def place(number):
+        half, chip = divmod(number, chips)
+        x_in = X // row
+        return chip // (x_in * Z), chip // x_in % Z, half * x_in + chip % x_in
+
+    def apart(number):
+        y, z, x = place(number)
+        along = abs(z - LEAD[1])
+        return abs(y - LEAD[0]) + min(along, Z - along) + abs(x - LEAD[2])
+
+    return sorted(range(row * chips), key=lambda number: (apart(number) > 0, -apart(number)))
+
+
+def chip_groups(order, row):
+    chips = len(order) // row
     return [
-        [(chip * 2 + core) * row + half for half in range(row) for chip in range(chips)]
+        [(number % chips * 2 + core) * row + number // chips for number in order]
         for core in range(2)
     ]
 
@@ -112,7 +132,7 @@
 
 
 def own_kernel(
-    got_ref, normed_ref, gate_ref, w_out_ref, left_ref, own_ref, gating_ref, held_out_ref
+    seats, got_ref, normed_ref, gate_ref, w_out_ref, left_ref, own_ref, gating_ref, held_out_ref
 ):
     held_out_ref[...] = w_out_ref[...]
     blocks, both, cols = got_ref.shape
@@ -120,10 +140,10 @@
     size = chips * rows
     own = jnp.zeros((size, size), jnp.float32)
     for half in range(2):
-        part = pl.ds(half * chips, chips)
-        left = flat(got_ref[part, :rows, :])
+        got = jnp.stack([got_ref[seat] for seat in seats[half * chips : (half + 1) * chips]])
+        left = flat(got[:, :rows, :])
         left_ref[half] = left
-        own += dot_rows(left, flat(got_ref[part, rows:, :]))
+        own += dot_rows(left, flat(got[:, rows:, :]))
     own = own.astype(jnp.bfloat16)
     order = column_order(lax.axis_index("wide") % 2, rows, cols)
     for half in range(2):
@@ -134,11 +154,11 @@
     )
 
 
-def own_part(got, normed, w_gate, w_out):
+def own_part(seats, got, normed, w_gate, w_out):
     blocks, both, cols = got.shape
     size = blocks // 2 * (both // 2)
     return pl.pallas_call(
-        own_kernel,
+        functools.partial(own_kernel, seats),
         out_shape=(
             jax.ShapeDtypeStruct((2, size, cols), jnp.bfloat16),
             jax.ShapeDtypeStruct((2, size, cols), jnp.float32),
@@ -154,13 +174,14 @@
     )(got, normed, w_gate, w_out)
 
 
-def plane_kernel(other_ref, left_ref, own_ref, out_ref):
+def plane_kernel(seats, other_ref, left_ref, own_ref, out_ref):
     blocks, rows, cols = out_ref.shape
     chips = blocks // 2
     size = chips * rows
     other = jnp.zeros((size, size), jnp.float32)
     for half in range(2):
-        other += dot_rows(left_ref[half], flat(other_ref[pl.ds(half * chips, chips)]))
+        part = seats[half * chips : (half + 1) * chips]
+        other += dot_rows(left_ref[half], flat(jnp.stack([other_ref[seat] for seat in part])))
     other = other.astype(jnp.bfloat16)
     order = column_order(1 - lax.axis_index("wide") % 2, rows, cols)
     for half in range(2):
@@ -168,14 +189,14 @@
         placed = own_ref[half] + jnp.dot(
             other[:, span], order, preferred_element_type=jnp.float32
         )
-        out_ref[pl.ds(half * chips, chips)] = placed.reshape(chips, rows, cols).astype(
-            jnp.bfloat16
-        )
-
-
-def plane_blocks(other, left, own):
-    return pl.pallas_call(
-        plane_kernel,
+        blocks_back = placed.reshape(chips, rows, cols).astype(jnp.bfloat16)
+        for chip in range(chips):
+            out_ref[seats[half * chips + chip]] = blocks_back[chip]
+
+
+def plane_blocks(seats, other, left, own):
+    return pl.pallas_call(
+        functools.partial(plane_kernel, seats),
         out_shape=jax.ShapeDtypeStruct(other.shape, jnp.bfloat16),
         in_specs=[VMEM] * 3,
         out_specs=VMEM,
@@ -220,7 +241,9 @@
 
 
 def make(wide, row):
-    groups = chip_groups(wide, row)
+    order = group_order(wide // 2, row)
+    groups = chip_groups(order, row)
+    seats = [order.index(number) for number in range(len(order))]
 
     def shards(pair, token_valid, w_pair, w_gate, w_out):
         rows = pair.shape[0]
@@ -228,8 +251,8 @@
         sent = project_blocks(normed, token_valid, w_pair, rows, w_out.shape[0])
         got = exchange(sent, groups)
         other = lax.ppermute(got[:, rows:, :], "wide", [(i, i ^ 1) for i in range(wide)])
-        left, own, gating, w_out = own_part(got, normed, w_gate, w_out)
-        returned = exchange(plane_blocks(other, left, own), groups)
+        left, own, gating, w_out = own_part(seats, got, normed, w_gate, w_out)
+        returned = exchange(plane_blocks(seats, other, left, own), groups)
         return finish(returned, gating, w_out, pair.shape)
 
     return shards

time: 61.8 us -> 55.9 us (0.905); the launches traced: 60.6 us -> 55.6 us
  blocking collectives: 52.3 us -> 48.3 us
  starting transfers between devices: 2.76 us -> 1.73 us
    all_to_all x2, blocking collectives: 52.3 us -> 48.3 us  [exchange(): lax.all_to_all(blocks, ('wide', 'row'), split_axis=0, concat_axis=0, tile...]
    ppermute x1, starting transfers between devices: 2.76 us -> 1.73 us  [shards(): lax.ppermute(got[:, rows:, :], 'wide', [(i, i ^ 1) for i in range(wide)])]
where the time goes in v6:
time: 55.9 us; the launch traced here: 55.6 us
  blocking collectives  48.3 us (86%)
  Pallas kernels  3.64 us (7%)
  starting transfers between devices  1.73 us (3%)
  local copies, waits for them, and re-layouts  1.39 us (2%)
    all_to_all x2, blocking collectives, exchange(): lax.all_to_all(blocks, ('wide', 'row'), split_axis=0, concat_axis=0, tile...  48.3 us
    ppermute x1, starting transfers between devices, shards(): lax.ppermute(got[:, rows:, :], 'wide', [(i, i ^ 1) for i in range(wide)])  1.73 us
    unnamed x10, local copies, waits for them, and re-layouts  1.25 us
    pallas_call x1, Pallas kernels, finish(): pl.pallas_call(finish_kernel, out_shape=jax.ShapeDtypeStruct(shape, jnp.b...  1.24 us
  transfers between devices with their start and end apart: 1, of which 1 were waited for; matrix products, arithmetic and copies ran while one was open for 0% of the time, Pallas kernels for 1%

profile of v6, /device:TPU:1, one launch (start us, length us, event | category | flops | bytes accessed | tf_op | source)
XLA Modules:
  0.0 55.6 jit_solution(3520092587016441210)
XLA Ops:
  0.0 0.0 copy-start
  0.0 0.9 %copy-done = bf16[4,256,128]{2,1,0:T(8,128)(2,1)S(1)} copy-done((bf16[4,256,128]{2,1,0:T(8,128)(2,1)S(1)}, bf16[4,256,128]{2,1,0:T(8,128)(2,1)}, u32[]{:S(2)}) %copy-start) | copy-done | bytes 262168
  1.0 0.0 copy-start.1
  1.0 0.0 copy-start.4
  1.0 0.6 %shard_map.55.normed_ref = bf16[1024,128]{1,0:T(8,128)(2,1)S(1)} custom-call(bf16[4,256,128]{2,1,0:T(8,128)(2,1)S(1)} %copy-done), custom_call_target="tpu_custom_call" | custom-call | flops 134217728 | bytes 4194304 | tf_op jit(solution)/shard_map/pallas_call | solution.py:78
  1.6 0.3 copy-done.1
  1.9 0.0 copy-done.4
  1.9 0.6 %shard_map.56 = bf16[128,8,256]{2,1,0:T(8,128)(2,1)S(1)} custom-call(bf16[1024,128]{1,0:T(8,128)(2,1)S(1)} %shard_map.55.normed_ref, s32[1,512]{1,0:T(1,128)S(1)} %bitcast.1, bf16[128,512]{1,0:T(8,128)(2,1)S(1)} %copy-done.1), custom_call_target="tpu_custom_call" | custom-call | tf_op jit(solution)/shard_map/pallas_call | solution.py:112
  2.5 29.0 %all_to_all.10.got_ref = bf16[128,8,256]{2,1,0:T(8,128)(2,1)S(1)} all-to-all(bf16[128,8,256]{2,1,0:T(8,128)(2,1)S(1)} %shard_map.56), channel_id=1, replica_groups={{169,8,0,12,16,72,200,13,4,20,24,56,64,76,80,136,192,204,208,5,9,21,77,..., dimensions={0} | all-to-all | bytes 1048576 | tf_op jit(solution)/shard_map/all_to_all | solution.py:42
  31.5 0.0 copy-start.2
  31.5 0.0 copy-start.3
  31.5 0.1 slice.4
  31.7 1.7 %collective-permute-start = (bf16[128,4,256]{2,1,0:T(4,128)(2,1)S(1)}, bf16[128,4,256]{2,1,0:T(4,128)(2,1)S(1)}, u32[]{:S(2)}, u32[]{:S(2)}) collective-permute-start(bf16[128,4,256]{2,1,0:T(4,128)(2,1)S(1)} %slice.4), channel_id=1, source_target_pairs={{0,2},{2,0},{4,6},{6,4},{8,10},{10,8},{12,14},{14,12},{16,18},{18,... | collective-permute-start | bytes 786440 | tf_op jit(solution)/shard_map/ppermute | solution.py:253
  33.4 0.0 copy-done.2
  33.4 0.0 copy-done.3
  33.4 0.7 %shard_map.57 = (bf16[2,256,256]{2,1,0:T(8,128)(2,1)S(1)}, f32[2,256,256]{2,1,0:T(8,128)S(1)}, f32[1024,128]{1,0:T(8,128)S(1)}, bf16[128,128]{1,0:T(8,128)(2,1)S(1)}) custom-call(bf16[128,8,256]{2,1,0:T(8,128)(2,1)S(1)} %all_to_all.10.got_ref, bf16[1024,128]{1,0:T(8,128)(2,1)S(1)} %shard_map.55.normed_ref, bf16[128,128]{1,0:T(8,128)(2,1)S(1)} %copy-done.2, ...), custom_call_target="tpu_custom_call" | custom-call | flops 67108864 | bytes 3145728 | tf_op jit(solution)/shard_map/pallas_call | solution.py:160
  34.1 0.5 collective-permute-done.other_ref
  34.6 0.5 shard_map.58
  35.1 19.3 %all_to_all.11.returned_ref = bf16[128,4,256]{2,1,0:T(4,128)(2,1)S(1)} all-to-all(bf16[128,4,256]{2,1,0:T(4,128)(2,1)S(1)} %shard_map.58), channel_id=1, replica_groups={{169,8,0,12,16,72,200,13,4,20,24,56,64,76,80,136,192,204,208,5,9,21,77,..., dimensions={0} | all-to-all | bytes 524288 | tf_op jit(solution)/shard_map/all_to_all | solution.py:42
  54.4 1.2 %shard_map.59 = bf16[4,256,128]{2,1,0:T(8,128)(2,1)} custom-call(bf16[128,4,256]{2,1,0:T(4,128)(2,1)S(1)} %all_to_all.11.returned_ref, f32[1024,128]{1,0:T(8,128)S(1)} %get-tuple-element.11.gating_ref, bf16[128,128]{1,0:T(8,128)(2,1)S(1)} %get-tuple-element.12.out_ref), custom_call_target="tpu_custom_call" | custom-call | tf_op jit(solution)/shard_map/pallas_call | solution.py:230
Async XLA Ops:
  0.0 0.9 %copy-start = (bf16[4,256,128]{2,1,0:T(8,128)(2,1)S(1)}, bf16[4,256,128]{2,1,0:T(8,128)(2,1)}, u32[]{:S(2)}) copy-start(bf16[4,256,128]{2,1,0:T(8,128)(2,1)} %pair_ref.1) | copy-start | bytes 786436
  1.0 0.9 %copy-start.1 = (bf16[128,512]{1,0:T(8,128)(2,1)S(1)}, bf16[128,512]{1,0:T(8,128)(2,1)}, u32[]{:S(2)}) copy-start(bf16[128,512]{1,0:T(8,128)(2,1)} %w_ref.1) | copy-start | bytes 393220
  1.0 0.9 %copy-start.4 = (s32[512]{0:T(512)S(1)}, s32[512]{0:T(512)}, u32[]{:S(2)}) copy-start(s32[512]{0:T(512)} %param.6) | copy-start | bytes 6148
  31.5 1.9 %copy-start.2 = (bf16[128,128]{1,0:T(8,128)(2,1)S(1)}, bf16[128,128]{1,0:T(8,128)(2,1)}, u32[]{:S(2)}) copy-start(bf16[128,128]{1,0:T(8,128)(2,1)} %gate_ref.1) | copy-start | bytes 98308
  31.5 1.9 %copy-start.3 = (bf16[128,128]{1,0:T(8,128)(2,1)S(1)}, bf16[128,128]{1,0:T(8,128)(2,1)}, u32[]{:S(2)}) copy-start(bf16[128,128]{1,0:T(8,128)(2,1)} %w_out_ref.1) | copy-start | bytes 98308
  31.7 2.9 %collective-permute-start = (bf16[128,4,256]{2,1,0:T(4,128)(2,1)S(1)}, bf16[128,4,256]{2,1,0:T(4,128)(2,1)S(1)}, u32[]{:S(2)}, u32[]{:S(2)}) collective-permute-start(bf16[128,4,256]{2,1,0:T(4,128)(2,1)S(1)} %slice.4), channel_id=1, source_target_pairs={{0,2},{2,0},{4,6},{6,4},{8,10},{10,8},{12,14},{14,12},{16,18},{18,... | collective-permute-start | bytes 786440 | tf_op jit(solution)/shard_map/ppermute | solution.py:253

commit v7 on v6

--- a/solution.py
+++ b/solution.py
@@ -56,18 +56,18 @@
 
 def normed_kernel(pair_ref, normed_ref):
     rows, cols, width = pair_ref.shape
-    ones = jnp.ones((width, width), jnp.bfloat16)
-
-    def total(values):
-        return jnp.dot(values, ones, preferred_element_type=jnp.float32)
+    share = jnp.full((2 * width, width), 1.0 / width, jnp.bfloat16)
+
+    def mean(values):
+        return jnp.dot(values, share[: values.shape[1]], preferred_element_type=jnp.float32)
 
     for row in range(rows):
         values = pair_ref[row]
-        centered = values.astype(jnp.float32) - total(values) * (1.0 / width)
+        centered = values.astype(jnp.float32) - mean(values)
         square = centered * centered
         high = square.astype(jnp.bfloat16)
         low = (square - high.astype(jnp.float32)).astype(jnp.bfloat16)
-        spread = (total(high) + total(low)) * (1.0 / width)
+        spread = mean(jnp.concatenate([high, low], axis=1))
         normed_ref[pl.ds(row * cols, cols), :] = (
             centered * lax.rsqrt(spread + 1e-05)
         ).astype(jnp.bfloat16)
@@ -99,12 +99,14 @@
         row_valid = jnp.sum(jnp.where(seat == first + row, valid, 0.0), axis=1, keepdims=True)
         mask = row_valid * col_valid
         proj = dot_rows(turned, normed_ref[pl.ds(row * cols, cols), :])
-        held[row] = sigmoid(proj[:hidden]) * proj[hidden : 2 * hidden] * mask
-        held[rows + row] = sigmoid(proj[2 * hidden : 3 * hidden]) * proj[3 * hidden :] * mask
+        left = sigmoid(proj[:hidden]) * proj[hidden : 2 * hidden] * mask
+        right = sigmoid(proj[2 * hidden : 3 * hidden]) * proj[3 * hidden :] * mask
+        held[row] = left.astype(jnp.bfloat16)
+        held[rows + row] = right.astype(jnp.bfloat16)
     step = 16
     for first_channel in range(0, hidden, step):
         part = slice(first_channel, first_channel + step)
-        sent_ref[part] = jnp.transpose(held[:, part, :], (1, 0, 2)).astype(jnp.bfloat16)
+        sent_ref[part] = jnp.transpose(held[:, part, :], (1, 0, 2))
 
 
 def project_blocks(normed, token_valid, w_pair, rows, hidden):
@@ -114,7 +116,7 @@
         out_shape=jax.ShapeDtypeStruct((hidden, 2 * rows, cols), jnp.bfloat16),
         in_specs=[VMEM] * 3,
         out_specs=VMEM,
-        scratch_shapes=[pltpu.VMEM((2 * rows, hidden, cols), jnp.float32)],
+        scratch_shapes=[pltpu.VMEM((2 * rows, hidden, cols), jnp.bfloat16)],
         compiler_params=ROOM,
     )(normed, token_valid.reshape(1, -1), w_pair)
 
@@ -122,13 +124,6 @@
 def flat(values):
     chips, rows, cols = values.shape
     return values.astype(jnp.float32).reshape(chips * rows, cols).astype(jnp.bfloat16)
-
-
-def column_order(core, rows, cols):
-    source = lax.broadcasted_iota(jnp.int32, (cols // 2, cols), 0)
-    target = lax.broadcasted_iota(jnp.int32, (cols // 2, cols), 1)
-    place = (source // rows * 2 + core) * rows + source % rows
-    return jnp.where(place == target, 1.0, 0.0).astype(jnp.bfloat16)
 
 
 def own_kernel(
@@ -137,18 +132,11 @@
     held_out_ref[...] = w_out_ref[...]
     blocks, both, cols = got_ref.shape
     rows, chips = both // 2, blocks // 2
-    size = chips * rows
-    own = jnp.zeros((size, size), jnp.float32)
     for half in range(2):
-        got = jnp.stack([got_ref[seat] for seat in seats[half * chips : (half + 1) * chips]])
-        left = flat(got[:, :rows, :])
-        left_ref[half] = left
-        own += dot_rows(left, flat(got[:, rows:, :]))
-    own = own.astype(jnp.bfloat16)
-    order = column_order(lax.axis_index("wide") % 2, rows, cols)
-    for half in range(2):
-        span = slice(half * (size // 2), (half + 1) * (size // 2))
-        own_ref[half] = jnp.dot(own[:, span], order, preferred_element_type=jnp.float32)
+        part = seats[half * chips : (half + 1) * chips]
+        got = jnp.stack([got_ref[seat] for seat in part])
+        left_ref[half] = flat(got[:, :rows, :])
+        own_ref[half] = got[:, rows:, :].astype(jnp.float32)
     gating_ref[...] = sigmoid(
         jnp.dot(normed_ref[...], gate_ref[...], preferred_element_type=jnp.float32)
     )
@@ -156,12 +144,12 @@
 
 def own_part(seats, got, normed, w_gate, w_out):
     blocks, both, cols = got.shape
-    size = blocks // 2 * (both // 2)
+    rows, chips = both // 2, blocks // 2
     return pl.pallas_call(
         functools.partial(own_kernel, seats),
         out_shape=(
-            jax.ShapeDtypeStruct((2, size, cols), jnp.bfloat16),
-            jax.ShapeDtypeStruct((2, size, cols), jnp.float32),
+            jax.ShapeDtypeStruct((2, chips * rows, cols), jnp.bfloat16),
+            jax.ShapeDtypeStruct((2, chips, rows, cols), jnp.float32),
             jax.ShapeDtypeStruct(normed.shape, jnp.float32),
             jax.ShapeDtypeStruct(w_out.shape, jnp.bfloat16),
         ),
@@ -169,35 +157,37 @@
         out_specs=(VMEM,) * 4,
         compiler_params=ROOM,
         cost_estimate=pl.CostEstimate(
-            flops=4 * size * size * cols, bytes_accessed=3 * 1024 * 1024, transcendentals=0
+            flops=4 * (chips * rows) ** 2 * cols, bytes_accessed=3 * 1024 * 1024, transcendentals=0
         ),
     )(got, normed, w_gate, w_out)
 
 
 def plane_kernel(seats, other_ref, left_ref, own_ref, out_ref):
-    blocks, rows, cols = out_ref.shape
+    blocks, rows, cols = other_ref.shape
     chips = blocks // 2
-    size = chips * rows
-    other = jnp.zeros((size, size), jnp.float32)
+    plane = jnp.zeros((chips * rows, 2 * chips * rows), jnp.float32)
+    first = lax.axis_index("wide") % 2 == 0
     for half in range(2):
         part = seats[half * chips : (half + 1) * chips]
-        other += dot_rows(left_ref[half], flat(jnp.stack([other_ref[seat] for seat in part])))
-    other = other.astype(jnp.bfloat16)
-    order = column_order(1 - lax.axis_index("wide") % 2, rows, cols)
+        own = own_ref[half]
+        other = jnp.stack([other_ref[seat] for seat in part]).astype(jnp.float32)
+        right = jnp.concatenate(
+            [jnp.where(first, own, other), jnp.where(first, other, own)], axis=1
+        )
+        plane += dot_rows(left_ref[half], right.reshape(-1, cols).astype(jnp.bfloat16))
     for half in range(2):
-        span = slice(half * (size // 2), (half + 1) * (size // 2))
-        placed = own_ref[half] + jnp.dot(
-            other[:, span], order, preferred_element_type=jnp.float32
-        )
-        blocks_back = placed.reshape(chips, rows, cols).astype(jnp.bfloat16)
+        placed = plane[:, half * cols : (half + 1) * cols].reshape(chips, rows, cols)
+        tiles = jnp.concatenate([placed[:, :, : cols // 2], placed[:, :, cols // 2 :]], axis=1)
+        tiles = tiles.astype(jnp.bfloat16)
         for chip in range(chips):
-            out_ref[seats[half * chips + chip]] = blocks_back[chip]
+            out_ref[seats[half * chips + chip]] = tiles[chip]
 
 
 def plane_blocks(seats, other, left, own):
+    blocks, rows, cols = other.shape
     return pl.pallas_call(
         functools.partial(plane_kernel, seats),
-        out_shape=jax.ShapeDtypeStruct(other.shape, jnp.bfloat16),
+        out_shape=jax.ShapeDtypeStruct((blocks, 2 * rows, cols // 2), jnp.bfloat16),
         in_specs=[VMEM] * 3,
         out_specs=VMEM,
         compiler_params=ROOM,
@@ -207,10 +197,10 @@
 def finish_kernel(returned_ref, gating_ref, out_ref, update_hbm, staged, left_device):
     rows, cols, width = staged.shape
     hidden = returned_ref.shape[0]
-    turned = jnp.transpose(returned_ref[...].astype(jnp.float32), (1, 0, 2))
+    turned = jnp.transpose(returned_ref[...], (1, 0, 2))
     copies = []
     for row in range(rows):
-        values = turned[row]
+        values = jnp.concatenate([turned[row], turned[rows + row]], axis=1).astype(jnp.float32)
         mean = jnp.sum(values, axis=0, keepdims=True) * (1.0 / hidden)
         centered = values - mean
         spread = jnp.sum(centered * centered, axis=0, keepdims=True) * (1.0 / hidden)

time: 55.9 us -> 55.5 us (level)
  Pallas kernels: 3.64 us -> 2.87 us
where the time goes in v7:
time: 55.5 us; the launch traced here: 55.2 us
  blocking collectives  48.3 us (87%)
  Pallas kernels  2.87 us (5%)
  starting transfers between devices  1.73 us (3%)
  local copies, waits for them, and re-layouts  1.42 us (3%)
  waiting for transfers between devices  0.84 us (2%)
    all_to_all x2, blocking collectives, exchange(): lax.all_to_all(blocks, ('wide', 'row'), split_axis=0, concat_axis=0, tile...  48.3 us
    ppermute x1, starting transfers between devices, shards(): lax.ppermute(got[:, rows:, :], 'wide', [(i, i ^ 1) for i in range(wide)])  1.73 us
    unnamed x10, local copies, waits for them, and re-layouts  1.28 us
  transfers between devices with their start and end apart: 1, of which 1 were waited for; matrix products, arithmetic and copies ran while one was open for 0% of the time, Pallas kernels for 1%

profile of v7, /device:TPU:1, one launch (start us, length us, event | category | flops | bytes accessed | tf_op | source)
XLA Modules:
  0.0 55.2 jit_solution(17348999021825728522)
XLA Ops:
  0.0 0.0 copy-start
  0.0 0.9 %copy-done = bf16[4,256,128]{2,1,0:T(8,128)(2,1)S(1)} copy-done((bf16[4,256,128]{2,1,0:T(8,128)(2,1)S(1)}, bf16[4,256,128]{2,1,0:T(8,128)(2,1)}, u32[]{:S(2)}) %copy-start) | copy-done | bytes 262168
  1.0 0.0 copy-start.1
  1.0 0.0 copy-start.4
  1.0 0.6 %shard_map.55.normed_ref = bf16[1024,128]{1,0:T(8,128)(2,1)S(1)} custom-call(bf16[4,256,128]{2,1,0:T(8,128)(2,1)S(1)} %copy-done), custom_call_target="tpu_custom_call" | custom-call | flops 134217728 | bytes 4194304 | tf_op jit(solution)/shard_map/pallas_call | solution.py:78
  1.5 0.3 copy-done.1
  1.9 0.0 copy-done.4
  1.9 0.6 %shard_map.56 = bf16[128,8,256]{2,1,0:T(8,128)(2,1)S(1)} custom-call(bf16[1024,128]{1,0:T(8,128)(2,1)S(1)} %shard_map.55.normed_ref, s32[1,512]{1,0:T(1,128)S(1)} %bitcast.1, bf16[128,512]{1,0:T(8,128)(2,1)S(1)} %copy-done.1), custom_call_target="tpu_custom_call" | custom-call | tf_op jit(solution)/shard_map/pallas_call | solution.py:114
  2.4 29.0 %all_to_all.10.got_ref = bf16[128,8,256]{2,1,0:T(8,128)(2,1)S(1)} all-to-all(bf16[128,8,256]{2,1,0:T(8,128)(2,1)S(1)} %shard_map.56), channel_id=1, replica_groups={{169,8,0,12,16,72,200,13,4,20,24,56,64,76,80,136,192,204,208,5,9,21,77,..., dimensions={0} | all-to-all | bytes 1048576 | tf_op jit(solution)/shard_map/all_to_all | solution.py:42
  31.5 0.0 copy-start.2
  31.5 0.0 copy-start.3
  31.5 0.1 slice.4
  31.6 1.7 %collective-permute-start = (bf16[128,4,256]{2,1,0:T(4,128)(2,1)S(1)}, bf16[128,4,256]{2,1,0:T(4,128)(2,1)S(1)}, u32[]{:S(2)}, u32[]{:S(2)}) collective-permute-start(bf16[128,4,256]{2,1,0:T(4,128)(2,1)S(1)} %slice.4), channel_id=1, source_target_pairs={{0,2},{2,0},{4,6},{6,4},{8,10},{10,8},{12,14},{14,12},{16,18},{18,... | collective-permute-start | bytes 786440 | tf_op jit(solution)/shard_map/ppermute | solution.py:243
  33.4 0.0 copy-done.2
  33.4 0.0 copy-done.3
  33.4 0.3 shard_map.57
  33.7 0.8 %collective-permute-done.other_ref = bf16[128,4,256]{2,1,0:T(4,128)(2,1)S(1)} collective-permute-done((bf16[128,4,256]{2,1,0:T(4,128)(2,1)S(1)}, bf16[128,4,256]{2,1,0:T(4,128)(2,1)S(1)}, u32[]{:S(2)}, u32[]{:S(2)}) %collective-permute-start) | collective-permute-done | bytes 262176 | tf_op jit(solution)/shard_map/ppermute | solution.py:243
  34.5 0.4 shard_map.58
  34.9 19.3 %all_to_all.11.returned_ref = bf16[128,8,128]{2,1,0:T(8,128)(2,1)S(1)} all-to-all(bf16[128,8,128]{2,1,0:T(8,128)(2,1)S(1)} %shard_map.58), channel_id=1, replica_groups={{169,8,0,12,16,72,200,13,4,20,24,56,64,76,80,136,192,204,208,5,9,21,77,..., dimensions={0} | all-to-all | bytes 524288 | tf_op jit(solution)/shard_map/all_to_all | solution.py:42
  54.1 1.1 %shard_map.59 = bf16[4,256,128]{2,1,0:T(8,128)(2,1)} custom-call(bf16[128,8,128]{2,1,0:T(8,128)(2,1)S(1)} %all_to_all.11.returned_ref, f32[1024,128]{1,0:T(8,128)S(1)} %get-tuple-element.11.gating_ref, bf16[128,128]{1,0:T(8,128)(2,1)S(1)} %get-tuple-element.12.out_ref), custom_call_target="tpu_custom_call" | custom-call | tf_op jit(solution)/shard_map/pallas_call | solution.py:220
Async XLA Ops:
  0.0 0.9 %copy-start = (bf16[4,256,128]{2,1,0:T(8,128)(2,1)S(1)}, bf16[4,256,128]{2,1,0:T(8,128)(2,1)}, u32[]{:S(2)}) copy-start(bf16[4,256,128]{2,1,0:T(8,128)(2,1)} %pair_ref.1) | copy-start | bytes 786436
  1.0 0.9 %copy-start.1 = (bf16[128,512]{1,0:T(8,128)(2,1)S(1)}, bf16[128,512]{1,0:T(8,128)(2,1)}, u32[]{:S(2)}) copy-start(bf16[128,512]{1,0:T(8,128)(2,1)} %w_ref.1) | copy-start | bytes 393220
  1.0 0.9 %copy-start.4 = (s32[512]{0:T(512)S(1)}, s32[512]{0:T(512)}, u32[]{:S(2)}) copy-start(s32[512]{0:T(512)} %param.6) | copy-start | bytes 6148
  31.5 1.9 %copy-start.2 = (bf16[128,128]{1,0:T(8,128)(2,1)S(1)}, bf16[128,128]{1,0:T(8,128)(2,1)}, u32[]{:S(2)}) copy-start(bf16[128,128]{1,0:T(8,128)(2,1)} %gate_ref.1) | copy-start | bytes 98308
  31.5 1.9 %copy-start.3 = (bf16[128,128]{1,0:T(8,128)(2,1)S(1)}, bf16[128,128]{1,0:T(8,128)(2,1)}, u32[]{:S(2)}) copy-start(bf16[128,128]{1,0:T(8,128)(2,1)} %w_out_ref.1) | copy-start | bytes 98308
  31.6 2.9 %collective-permute-start = (bf16[128,4,256]{2,1,0:T(4,128)(2,1)S(1)}, bf16[128,4,256]{2,1,0:T(4,128)(2,1)S(1)}, u32[]{:S(2)}, u32[]{:S(2)}) collective-permute-start(bf16[128,4,256]{2,1,0:T(4,128)(2,1)S(1)} %slice.4), channel_id=1, source_target_pairs={{0,2},{2,0},{4,6},{6,4},{8,10},{10,8},{12,14},{14,12},{16,18},{18,... | collective-permute-start | bytes 786440 | tf_op jit(solution)/shard_map/ppermute | solution.py:243

commit v8 on v7

--- a/solution.py
+++ b/solution.py
@@ -9,6 +9,7 @@
 
 VMEM = pl.BlockSpec(memory_space=pltpu.VMEM)
 ANY = pl.BlockSpec(memory_space=pl.ANY)
+HBM = pl.BlockSpec(memory_space=pltpu.HBM)
 ROOM = pltpu.CompilerParams(vmem_limit_bytes=32 * 1024 * 1024)
 
 
@@ -54,43 +55,84 @@
     return 0.5 * jnp.tanh(0.5 * values) + 0.5
 
 
-def normed_kernel(pair_ref, normed_ref):
+def weights_kernel(w_hbm, valid_hbm, share_ref, turned_ref, valid_ref, w_ref, arrived):
+    part = w_ref.shape[0] // 4
+    pieces = [
+        (w_hbm.at[pl.ds(at * part, part)], w_ref.at[pl.ds(at * part, part)]) for at in range(4)
+    ]
+    pieces += [(valid_hbm, valid_ref)]
+    copies = [
+        pltpu.make_async_copy(source, target, arrived.at[index])
+        for index, (source, target) in enumerate(pieces)
+    ]
+    for copy in copies:
+        copy.start()
+    share_ref[...] = jnp.full(share_ref.shape, 1.0 / share_ref.shape[1], jnp.bfloat16)
+    for copy in copies:
+        copy.wait()
+    turned_ref[...] = w_ref[...].T
+
+
+def prepare_weights(w_pair, valid):
+    width, outs = w_pair.shape
+    return pl.pallas_call(
+        weights_kernel,
+        out_shape=(
+            jax.ShapeDtypeStruct((2 * width, width), jnp.bfloat16),
+            jax.ShapeDtypeStruct((outs, width), jnp.bfloat16),
+            jax.ShapeDtypeStruct(valid.shape, jnp.int32),
+        ),
+        in_specs=[HBM] * 2,
+        out_specs=(VMEM,) * 3,
+        scratch_shapes=[
+            pltpu.VMEM(w_pair.shape, jnp.bfloat16),
+            pltpu.SemaphoreType.DMA((5,)),
+        ],
+        compiler_params=ROOM,
+        cost_estimate=pl.CostEstimate(
+            flops=1024**3, bytes_accessed=8 * 1024 * 1024, transcendentals=0
+        ),
+    )(*(pltpu.with_memory_space_constraint(value, pltpu.HBM) for value in (w_pair, valid)))
+
+
+def normed_kernel(pair_ref, share_ref, normed_ref):
     rows, cols, width = pair_ref.shape
-    share = jnp.full((2 * width, width), 1.0 / width, jnp.bfloat16)
 
     def mean(values):
-        return jnp.dot(values, share[: values.shape[1]], preferred_element_type=jnp.float32)
-
-    for row in range(rows):
-        values = pair_ref[row]
+        return jnp.dot(
+            values, share_ref[: values.shape[1], :], preferred_element_type=jnp.float32
+        )
+
+    step = rows // 2
+    for first in range(0, rows, step):
+        values = pair_ref[pl.ds(first, step)].reshape(step * cols, width)
         centered = values.astype(jnp.float32) - mean(values)
         square = centered * centered
         high = square.astype(jnp.bfloat16)
         low = (square - high.astype(jnp.float32)).astype(jnp.bfloat16)
         spread = mean(jnp.concatenate([high, low], axis=1))
-        normed_ref[pl.ds(row * cols, cols), :] = (
+        normed_ref[pl.ds(first * cols, step * cols), :] = (
             centered * lax.rsqrt(spread + 1e-05)
         ).astype(jnp.bfloat16)
 
 
-def norm_pair(pair):
+def norm_pair(pair, share):
     rows, cols, width = pair.shape
     return pl.pallas_call(
         normed_kernel,
         out_shape=jax.ShapeDtypeStruct((rows * cols, width), jnp.bfloat16),
-        in_specs=[VMEM],
+        in_specs=[VMEM] * 2,
         out_specs=VMEM,
         compiler_params=ROOM,
         cost_estimate=pl.CostEstimate(
             flops=8 * rows * cols * width * width, bytes_accessed=4 * 1024 * 1024, transcendentals=0
         ),
-    )(pair)
-
-
-def project_kernel(normed_ref, valid_ref, w_ref, sent_ref, held):
+    )(pair, share)
+
+
+def project_kernel(normed_ref, valid_ref, turned_ref, sent_ref, held):
     hidden, both, cols = sent_ref.shape
     rows = both // 2
-    turned = w_ref[...].T
     valid = valid_ref[...].astype(jnp.float32)
     seat = lax.broadcasted_iota(jnp.int32, valid.shape, 1)
     first = lax.axis_index("wide") * rows
@@ -98,7 +140,7 @@
     for row in range(rows):
         row_valid = jnp.sum(jnp.where(seat == first + row, valid, 0.0), axis=1, keepdims=True)
         mask = row_valid * col_valid
-        proj = dot_rows(turned, normed_ref[pl.ds(row * cols, cols), :])
+        proj = dot_rows(turned_ref[...], normed_ref[pl.ds(row * cols, cols), :])
         left = sigmoid(proj[:hidden]) * proj[hidden : 2 * hidden] * mask
         right = sigmoid(proj[2 * hidden : 3 * hidden]) * proj[3 * hidden :] * mask
         held[row] = left.astype(jnp.bfloat16)
@@ -109,7 +151,7 @@
         sent_ref[part] = jnp.transpose(held[:, part, :], (1, 0, 2))
 
 
-def project_blocks(normed, token_valid, w_pair, rows, hidden):
+def project_blocks(normed, valid, turned, rows, hidden):
     cols = normed.shape[0] // rows
     return pl.pallas_call(
         project_kernel,
@@ -118,7 +160,7 @@
         out_specs=VMEM,
         scratch_shapes=[pltpu.VMEM((2 * rows, hidden, cols), jnp.bfloat16)],
         compiler_params=ROOM,
-    )(normed, token_valid.reshape(1, -1), w_pair)
+    )(normed, valid, turned)
 
 
 def flat(values):
@@ -237,8 +279,9 @@
 
     def shards(pair, token_valid, w_pair, w_gate, w_out):
         rows = pair.shape[0]
-        normed = norm_pair(pair)
-        sent = project_blocks(normed, token_valid, w_pair, rows, w_out.shape[0])
+        share, turned, valid = prepare_weights(w_pair, token_valid.reshape(1, -1))
+        normed = norm_pair(pair, share)
+        sent = project_blocks(normed, valid, turned, rows, w_out.shape[0])
         got = exchange(sent, groups)
         other = lax.ppermute(got[:, rows:, :], "wide", [(i, i ^ 1) for i in range(wide)])
         left, own, gating, w_out = own_part(seats, got, normed, w_gate, w_out)

time: 55.5 us -> 55 us (level)
  local copies, waits for them, and re-layouts: 1.42 us -> 0.18 us
  Pallas kernels: 2.87 us -> 3.69 us
    unnamed x10 -> x6, local copies, waits for them, and re-layouts: 1.28 us -> 0.05 us
    pallas_call x0 -> x1, Pallas kernels: none -> 0.98 us  [prepare_weights(): pl.pallas_call(weights_kernel, out_shape=(jax.ShapeDtypeStruct((2 * width...]
where the time goes in v8:
time: 55 us; the launch traced here: 54.8 us
  blocking collectives  48.3 us (88%)
  Pallas kernels  3.69 us (7%)
  starting transfers between devices  1.71 us (3%)
  waiting for transfers between devices  0.84 us (2%)
    all_to_all x2, blocking collectives, exchange(): lax.all_to_all(blocks, ('wide', 'row'), split_axis=0, concat_axis=0, tile...  48.3 us
    ppermute x1, starting transfers between devices, shards(): lax.ppermute(got[:, rows:, :], 'wide', [(i, i ^ 1) for i in range(wide)])  1.71 us
  transfers between devices with their start and end apart: 1, of which 1 were waited for; matrix products, arithmetic and copies ran while one was open for 0% of the time, Pallas kernels for 1%

profile of v8, /device:TPU:1, one launch (start us, length us, event | category | flops | bytes accessed | tf_op | source)
XLA Modules:
  0.0 54.8 jit_solution(3182840086663898331)
XLA Ops:
  0.0 0.0 copy-start
  0.0 1.0 %shard_map.55 = (bf16[256,128]{1,0:T(8,128)(2,1)S(1)}, bf16[512,128]{1,0:T(8,128)(2,1)S(1)}, s32[1,512]{1,0:T(1,128)S(1)}) custom-call(bf16[128,512]{1,0:T(8,128)(2,1)} %w_hbm.1, s32[1,512]{1,0:T(1,128)} %bitcast.1), custom_call_target="tpu_custom_call" | custom-call | flops 1073741824 | bytes 8388608 | tf_op jit(solution)/shard_map/pallas_call | solution.py:78
  1.0 0.0 copy-done
  1.0 0.4 shard_map.56.normed_ref
  1.5 0.5 shard_map.57
  2.0 29.1 %all_to_all.10.got_ref = bf16[128,8,256]{2,1,0:T(8,128)(2,1)S(1)} all-to-all(bf16[128,8,256]{2,1,0:T(8,128)(2,1)S(1)} %shard_map.57), channel_id=1, replica_groups={{169,8,0,12,16,72,200,13,4,20,24,56,64,76,80,136,192,204,208,5,9,21,77,..., dimensions={0} | all-to-all | bytes 1048576 | tf_op jit(solution)/shard_map/all_to_all | solution.py:43
  31.1 0.0 copy-start.1
  31.1 0.0 copy-start.2
  31.1 0.1 slice.4
  31.2 1.7 %collective-permute-start = (bf16[128,4,256]{2,1,0:T(4,128)(2,1)S(1)}, bf16[128,4,256]{2,1,0:T(4,128)(2,1)S(1)}, u32[]{:S(2)}, u32[]{:S(2)}) collective-permute-start(bf16[128,4,256]{2,1,0:T(4,128)(2,1)S(1)} %slice.4), channel_id=1, source_target_pairs={{0,2},{2,0},{4,6},{6,4},{8,10},{10,8},{12,14},{14,12},{16,18},{18,... | collective-permute-start | bytes 786440 | tf_op jit(solution)/shard_map/ppermute | solution.py:286
  32.9 0.0 copy-done.1
  33.0 0.0 copy-done.2
  33.0 0.3 shard_map.58
  33.3 0.8 %collective-permute-done.other_ref = bf16[128,4,256]{2,1,0:T(4,128)(2,1)S(1)} collective-permute-done((bf16[128,4,256]{2,1,0:T(4,128)(2,1)S(1)}, bf16[128,4,256]{2,1,0:T(4,128)(2,1)S(1)}, u32[]{:S(2)}, u32[]{:S(2)}) %collective-permute-start) | collective-permute-done | bytes 262176 | tf_op jit(solution)/shard_map/ppermute | solution.py:286
  34.1 0.4 shard_map.59
  34.5 19.3 %all_to_all.11.returned_ref = bf16[128,8,128]{2,1,0:T(8,128)(2,1)S(1)} all-to-all(bf16[128,8,128]{2,1,0:T(8,128)(2,1)S(1)} %shard_map.59), channel_id=1, replica_groups={{169,8,0,12,16,72,200,13,4,20,24,56,64,76,80,136,192,204,208,5,9,21,77,..., dimensions={0} | all-to-all | bytes 524288 | tf_op jit(solution)/shard_map/all_to_all | solution.py:43
  53.7 1.1 %shard_map.60 = bf16[4,256,128]{2,1,0:T(8,128)(2,1)} custom-call(bf16[128,8,128]{2,1,0:T(8,128)(2,1)S(1)} %all_to_all.11.returned_ref, f32[1024,128]{1,0:T(8,128)S(1)} %get-tuple-element.17.gating_ref, bf16[128,128]{1,0:T(8,128)(2,1)S(1)} %get-tuple-element.18.out_ref), custom_call_target="tpu_custom_call" | custom-call | tf_op jit(solution)/shard_map/pallas_call | solution.py:262
Async XLA Ops:
  0.0 1.0 %copy-start = (bf16[4,256,128]{2,1,0:T(8,128)(2,1)S(1)}, bf16[4,256,128]{2,1,0:T(8,128)(2,1)}, u32[]{:S(2)}) copy-start(bf16[4,256,128]{2,1,0:T(8,128)(2,1)} %pair_ref.1) | copy-start | bytes 786436
  31.1 1.9 %copy-start.1 = (bf16[128,128]{1,0:T(8,128)(2,1)S(1)}, bf16[128,128]{1,0:T(8,128)(2,1)}, u32[]{:S(2)}) copy-start(bf16[128,128]{1,0:T(8,128)(2,1)} %gate_ref.1) | copy-start | bytes 98308
  31.1 1.9 %copy-start.2 = (bf16[128,128]{1,0:T(8,128)(2,1)S(1)}, bf16[128,128]{1,0:T(8,128)(2,1)}, u32[]{:S(2)}) copy-start(bf16[128,128]{1,0:T(8,128)(2,1)} %w_out_ref.1) | copy-start | bytes 98308
  31.2 2.9 %collective-permute-start = (bf16[128,4,256]{2,1,0:T(4,128)(2,1)S(1)}, bf16[128,4,256]{2,1,0:T(4,128)(2,1)S(1)}, u32[]{:S(2)}, u32[]{:S(2)}) collective-permute-start(bf16[128,4,256]{2,1,0:T(4,128)(2,1)S(1)} %slice.4), channel_id=1, source_target_pairs={{0,2},{2,0},{4,6},{6,4},{8,10},{10,8},{12,14},{14,12},{16,18},{18,... | collective-permute-start | bytes 786440 | tf_op jit(solution)/shard_map/ppermute | solution.py:286

commit v9 on v8

--- a/solution.py
+++ b/solution.py
@@ -52,7 +52,7 @@
 
 
 def sigmoid(values):
-    return 0.5 * jnp.tanh(0.5 * values) + 0.5
+    return 1.0 / (1.0 + jnp.exp(-values))
 
 
 def weights_kernel(w_hbm, valid_hbm, share_ref, turned_ref, valid_ref, w_ref, arrived):

time: 55 us -> 55 us (level)
  no operation moved by 1% of the time
where the time goes in v9:
time: 55 us; the launch traced here: 54.8 us
  blocking collectives  48.3 us (88%)
  Pallas kernels  3.78 us (7%)
  starting transfers between devices  1.71 us (3%)
  waiting for transfers between devices  0.77 us (1%)
    all_to_all x2, blocking collectives, exchange(): lax.all_to_all(blocks, ('wide', 'row'), split_axis=0, concat_axis=0, tile...  48.3 us
    ppermute x1, starting transfers between devices, shards(): lax.ppermute(got[:, rows:, :], 'wide', [(i, i ^ 1) for i in range(wide)])  1.71 us
  transfers between devices with their start and end apart: 1, of which 1 were waited for; matrix products, arithmetic and copies ran while one was open for 0% of the time, Pallas kernels for 1%

profile of v9, /device:TPU:1, one launch (start us, length us, event | category | flops | bytes accessed | tf_op | source)
XLA Modules:
  0.0 54.8 jit_solution(6503132127220365789)
XLA Ops:
  0.0 0.0 copy-start
  0.0 1.0 %shard_map.55 = (bf16[256,128]{1,0:T(8,128)(2,1)S(1)}, bf16[512,128]{1,0:T(8,128)(2,1)S(1)}, s32[1,512]{1,0:T(1,128)S(1)}) custom-call(bf16[128,512]{1,0:T(8,128)(2,1)} %w_hbm.1, s32[1,512]{1,0:T(1,128)} %bitcast.1), custom_call_target="tpu_custom_call" | custom-call | flops 1073741824 | bytes 8388608 | tf_op jit(solution)/shard_map/pallas_call | solution.py:78
  1.0 0.0 copy-done
  1.0 0.4 shard_map.56.normed_ref
  1.5 0.6 %shard_map.57 = bf16[128,8,256]{2,1,0:T(8,128)(2,1)S(1)} custom-call(bf16[1024,128]{1,0:T(8,128)(2,1)S(1)} %shard_map.56.normed_ref, s32[1,512]{1,0:T(1,128)S(1)} %get-tuple-element.13.valid_ref, bf16[512,128]{1,0:T(8,128)(2,1)S(1)} %get-tuple-element.14.turned_ref), custom_call_target="tpu_custom_call" | custom-call | tf_op jit(solution)/shard_map/pallas_call | solution.py:156
  2.0 29.1 %all_to_all.10.got_ref = bf16[128,8,256]{2,1,0:T(8,128)(2,1)S(1)} all-to-all(bf16[128,8,256]{2,1,0:T(8,128)(2,1)S(1)} %shard_map.57), channel_id=1, replica_groups={{169,8,0,12,16,72,200,13,4,20,24,56,64,76,80,136,192,204,208,5,9,21,77,..., dimensions={0} | all-to-all | bytes 1048576 | tf_op jit(solution)/shard_map/all_to_all | solution.py:43
  31.1 0.0 copy-start.1
  31.1 0.0 copy-start.2
  31.1 0.1 slice.4
  31.3 1.7 %collective-permute-start = (bf16[128,4,256]{2,1,0:T(4,128)(2,1)S(1)}, bf16[128,4,256]{2,1,0:T(4,128)(2,1)S(1)}, u32[]{:S(2)}, u32[]{:S(2)}) collective-permute-start(bf16[128,4,256]{2,1,0:T(4,128)(2,1)S(1)} %slice.4), channel_id=1, source_target_pairs={{0,2},{2,0},{4,6},{6,4},{8,10},{10,8},{12,14},{14,12},{16,18},{18,... | collective-permute-start | bytes 786440 | tf_op jit(solution)/shard_map/ppermute | solution.py:286
  33.0 0.0 copy-done.1
  33.0 0.0 copy-done.2
  33.0 0.4 shard_map.58
  33.4 0.8 %collective-permute-done.other_ref = bf16[128,4,256]{2,1,0:T(4,128)(2,1)S(1)} collective-permute-done((bf16[128,4,256]{2,1,0:T(4,128)(2,1)S(1)}, bf16[128,4,256]{2,1,0:T(4,128)(2,1)S(1)}, u32[]{:S(2)}, u32[]{:S(2)}) %collective-permute-start) | collective-permute-done | bytes 262176 | tf_op jit(solution)/shard_map/ppermute | solution.py:286
  34.1 0.4 shard_map.59
  34.5 19.3 %all_to_all.11.returned_ref = bf16[128,8,128]{2,1,0:T(8,128)(2,1)S(1)} all-to-all(bf16[128,8,128]{2,1,0:T(8,128)(2,1)S(1)} %shard_map.59), channel_id=1, replica_groups={{169,8,0,12,16,72,200,13,4,20,24,56,64,76,80,136,192,204,208,5,9,21,77,..., dimensions={0} | all-to-all | bytes 524288 | tf_op jit(solution)/shard_map/all_to_all | solution.py:43
  53.8 1.1 %shard_map.60 = bf16[4,256,128]{2,1,0:T(8,128)(2,1)} custom-call(bf16[128,8,128]{2,1,0:T(8,128)(2,1)S(1)} %all_to_all.11.returned_ref, f32[1024,128]{1,0:T(8,128)S(1)} %get-tuple-element.17.gating_ref, bf16[128,128]{1,0:T(8,128)(2,1)S(1)} %get-tuple-element.18.out_ref), custom_call_target="tpu_custom_call" | custom-call | tf_op jit(solution)/shard_map/pallas_call | solution.py:262
Async XLA Ops:
  0.0 1.0 %copy-start = (bf16[4,256,128]{2,1,0:T(8,128)(2,1)S(1)}, bf16[4,256,128]{2,1,0:T(8,128)(2,1)}, u32[]{:S(2)}) copy-start(bf16[4,256,128]{2,1,0:T(8,128)(2,1)} %pair_ref.1) | copy-start | bytes 786436
  31.1 1.9 %copy-start.1 = (bf16[128,128]{1,0:T(8,128)(2,1)S(1)}, bf16[128,128]{1,0:T(8,128)(2,1)}, u32[]{:S(2)}) copy-start(bf16[128,128]{1,0:T(8,128)(2,1)} %gate_ref.1) | copy-start | bytes 98308
  31.1 1.9 %copy-start.2 = (bf16[128,128]{1,0:T(8,128)(2,1)S(1)}, bf16[128,128]{1,0:T(8,128)(2,1)}, u32[]{:S(2)}) copy-start(bf16[128,128]{1,0:T(8,128)(2,1)} %w_out_ref.1) | copy-start | bytes 98308
  31.3 2.9 %collective-permute-start = (bf16[128,4,256]{2,1,0:T(4,128)(2,1)S(1)}, bf16[128,4,256]{2,1,0:T(4,128)(2,1)S(1)}, u32[]{:S(2)}, u32[]{:S(2)}) collective-permute-start(bf16[128,4,256]{2,1,0:T(4,128)(2,1)S(1)} %slice.4), channel_id=1, source_target_pairs={{0,2},{2,0},{4,6},{6,4},{8,10},{10,8},{12,14},{14,12},{16,18},{18,... | collective-permute-start | bytes 786440 | tf_op jit(solution)/shard_map/ppermute | solution.py:286

commit v10 on v9

--- a/solution.py
+++ b/solution.py
@@ -55,12 +55,15 @@
     return 1.0 / (1.0 + jnp.exp(-values))
 
 
-def weights_kernel(w_hbm, valid_hbm, share_ref, turned_ref, valid_ref, w_ref, arrived):
+def weights_kernel(
+    w_hbm, valid_hbm, gate_hbm, out_hbm,
+    share_ref, turned_ref, valid_ref, gate_ref, out_ref, w_ref, arrived,
+):
     part = w_ref.shape[0] // 4
     pieces = [
         (w_hbm.at[pl.ds(at * part, part)], w_ref.at[pl.ds(at * part, part)]) for at in range(4)
     ]
-    pieces += [(valid_hbm, valid_ref)]
+    pieces += [(valid_hbm, valid_ref), (gate_hbm, gate_ref), (out_hbm, out_ref)]
     copies = [
         pltpu.make_async_copy(source, target, arrived.at[index])
         for index, (source, target) in enumerate(pieces)
@@ -68,12 +71,14 @@
     for copy in copies:
         copy.start()
     share_ref[...] = jnp.full(share_ref.shape, 1.0 / share_ref.shape[1], jnp.bfloat16)
-    for copy in copies:
+    for copy in copies[:4]:
         copy.wait()
     turned_ref[...] = w_ref[...].T
-
-
-def prepare_weights(w_pair, valid):
+    for copy in copies[4:]:
+        copy.wait()
+
+
+def prepare_weights(w_pair, valid, w_gate, w_out):
     width, outs = w_pair.shape
     return pl.pallas_call(
         weights_kernel,
@@ -81,18 +86,25 @@
             jax.ShapeDtypeStruct((2 * width, width), jnp.bfloat16),
             jax.ShapeDtypeStruct((outs, width), jnp.bfloat16),
             jax.ShapeDtypeStruct(valid.shape, jnp.int32),
-        ),
-        in_specs=[HBM] * 2,
-        out_specs=(VMEM,) * 3,
+            jax.ShapeDtypeStruct(w_gate.shape, jnp.bfloat16),
+            jax.ShapeDtypeStruct(w_out.shape, jnp.bfloat16),
+        ),
+        in_specs=[HBM] * 4,
+        out_specs=(VMEM,) * 5,
         scratch_shapes=[
             pltpu.VMEM(w_pair.shape, jnp.bfloat16),
-            pltpu.SemaphoreType.DMA((5,)),
+            pltpu.SemaphoreType.DMA((7,)),
         ],
         compiler_params=ROOM,
         cost_estimate=pl.CostEstimate(
             flops=1024**3, bytes_accessed=8 * 1024 * 1024, transcendentals=0
         ),
-    )(*(pltpu.with_memory_space_constraint(value, pltpu.HBM) for value in (w_pair, valid)))
+    )(
+        *(
+            pltpu.with_memory_space_constraint(value, pltpu.HBM)
+            for value in (w_pair, valid, w_gate, w_out)
+        )
+    )
 
 
 def normed_kernel(pair_ref, share_ref, normed_ref):
@@ -168,10 +180,7 @@
     return values.astype(jnp.float32).reshape(chips * rows, cols).astype(jnp.bfloat16)
 
 
-def own_kernel(
-    seats, got_ref, normed_ref, gate_ref, w_out_ref, left_ref, own_ref, gating_ref, held_out_ref
-):
-    held_out_ref[...] = w_out_ref[...]
+def own_kernel(seats, got_ref, normed_ref, gate_ref, left_ref, own_ref, gating_ref):
     blocks, both, cols = got_ref.shape
     rows, chips = both // 2, blocks // 2
     for half in range(2):
@@ -184,7 +193,7 @@
     )
 
 
-def own_part(seats, got, normed, w_gate, w_out):
+def own_part(seats, got, normed, w_gate):
     blocks, both, cols = got.shape
     rows, chips = both // 2, blocks // 2
     return pl.pallas_call(
@@ -193,15 +202,14 @@
             jax.ShapeDtypeStruct((2, chips * rows, cols), jnp.bfloat16),
             jax.ShapeDtypeStruct((2, chips, rows, cols), jnp.float32),
             jax.ShapeDtypeStruct(normed.shape, jnp.float32),
-            jax.ShapeDtypeStruct(w_out.shape, jnp.bfloat16),
-        ),
-        in_specs=[VMEM] * 4,
-        out_specs=(VMEM,) * 4,
+        ),
+        in_specs=[VMEM] * 3,
+        out_specs=(VMEM,) * 3,
         compiler_params=ROOM,
         cost_estimate=pl.CostEstimate(
             flops=4 * (chips * rows) ** 2 * cols, bytes_accessed=3 * 1024 * 1024, transcendentals=0
         ),
-    )(got, normed, w_gate, w_out)
+    )(got, normed, w_gate)
 
 
 def plane_kernel(seats, other_ref, left_ref, own_ref, out_ref):
@@ -279,12 +287,14 @@
 
     def shards(pair, token_valid, w_pair, w_gate, w_out):
         rows = pair.shape[0]
-        share, turned, valid = prepare_weights(w_pair, token_valid.reshape(1, -1))
+        share, turned, valid, w_gate, w_out = prepare_weights(
+            w_pair, token_valid.reshape(1, -1), w_gate, w_out
+        )
         normed = norm_pair(pair, share)
         sent = project_blocks(normed, valid, turned, rows, w_out.shape[0])
         got = exchange(sent, groups)
         other = lax.ppermute(got[:, rows:, :], "wide", [(i, i ^ 1) for i in range(wide)])
-        left, own, gating, w_out = own_part(seats, got, normed, w_gate, w_out)
+        left, own, gating = own_part(seats, got, normed, w_gate)
         returned = exchange(plane_blocks(seats, other, left, own), groups)
         return finish(returned, gating, w_out, pair.shape)
 

time: 55 us -> 55 us (level)
  no operation moved by 1% of the time
where the time goes in v10:
time: 55 us; the launch traced here: 54.8 us
  blocking collectives  48.3 us (88%)
  Pallas kernels  3.79 us (7%)
  starting transfers between devices  1.71 us (3%)
  waiting for transfers between devices  0.78 us (1%)
    all_to_all x2, blocking collectives, exchange(): lax.all_to_all(blocks, ('wide', 'row'), split_axis=0, concat_axis=0, tile...  48.3 us
    ppermute x1, starting transfers between devices, shards(): lax.ppermute(got[:, rows:, :], 'wide', [(i, i ^ 1) for i in range(wide)])  1.71 us
  transfers between devices with their start and end apart: 1, of which 1 were waited for; matrix products, arithmetic and copies ran while one was open for 0% of the time, Pallas kernels for 1%

profile of v10, /device:TPU:1, one launch (start us, length us, event | category | flops | bytes accessed | tf_op | source)
XLA Modules:
  0.0 54.8 jit_solution(6477176923595229739)
XLA Ops:
  0.0 0.0 copy-start
  0.0 1.0 %shard_map.55 = (bf16[256,128]{1,0:T(8,128)(2,1)S(1)}, bf16[512,128]{1,0:T(8,128)(2,1)S(1)}, s32[1,512]{1,0:T(1,128)S(1)}, bf16[128,128]{1,0:T(8,128)(2,1)S(1)}, bf16[128,128]{1,0:T(8,128)(2,1)S(1)}) custom-call(bf16[128,512]{1,0:T(8,128)(2,1)} %w_hbm.1, s32[1,512]{1,0:T(1,128)} %bitcast.1, bf16[128,128]{1,0:T(8,128)(2,1)} %gate_hbm.1, bf16[128,128]{1,0:T(8,128)(2,1)} %out_hbm.1), custom_call_target="tpu_custom_call" | custom-call | flops 1073741824 | bytes 8388608 | tf_op jit(solution)/shard_map/pallas_call | solution.py:83
  1.0 0.0 copy-done
  1.1 0.4 shard_map.56.normed_ref
  1.5 0.6 %shard_map.57 = bf16[128,8,256]{2,1,0:T(8,128)(2,1)S(1)} custom-call(bf16[1024,128]{1,0:T(8,128)(2,1)S(1)} %shard_map.56.normed_ref, s32[1,512]{1,0:T(1,128)S(1)} %get-tuple-element.14.valid_ref, bf16[512,128]{1,0:T(8,128)(2,1)S(1)} %get-tuple-element.15.turned_ref), custom_call_target="tpu_custom_call" | custom-call | tf_op jit(solution)/shard_map/pallas_call | solution.py:168
  2.1 29.1 %all_to_all.10.got_ref = bf16[128,8,256]{2,1,0:T(8,128)(2,1)S(1)} all-to-all(bf16[128,8,256]{2,1,0:T(8,128)(2,1)S(1)} %shard_map.57), channel_id=1, replica_groups={{169,8,0,12,16,72,200,13,4,20,24,56,64,76,80,136,192,204,208,5,9,21,77,..., dimensions={0} | all-to-all | bytes 1048576 | tf_op jit(solution)/shard_map/all_to_all | solution.py:43
  31.1 0.1 slice.4
  31.3 1.7 %collective-permute-start = (bf16[128,4,256]{2,1,0:T(4,128)(2,1)S(1)}, bf16[128,4,256]{2,1,0:T(4,128)(2,1)S(1)}, u32[]{:S(2)}, u32[]{:S(2)}) collective-permute-start(bf16[128,4,256]{2,1,0:T(4,128)(2,1)S(1)} %slice.4), channel_id=1, source_target_pairs={{0,2},{2,0},{4,6},{6,4},{8,10},{10,8},{12,14},{14,12},{16,18},{18,... | collective-permute-start | bytes 786440 | tf_op jit(solution)/shard_map/ppermute | solution.py:296
  33.0 0.4 shard_map.58
  33.4 0.8 %collective-permute-done.other_ref = bf16[128,4,256]{2,1,0:T(4,128)(2,1)S(1)} collective-permute-done((bf16[128,4,256]{2,1,0:T(4,128)(2,1)S(1)}, bf16[128,4,256]{2,1,0:T(4,128)(2,1)S(1)}, u32[]{:S(2)}, u32[]{:S(2)}) %collective-permute-start) | collective-permute-done | bytes 262176 | tf_op jit(solution)/shard_map/ppermute | solution.py:296
  34.2 0.4 shard_map.59
  34.5 19.3 %all_to_all.11.returned_ref = bf16[128,8,128]{2,1,0:T(8,128)(2,1)S(1)} all-to-all(bf16[128,8,128]{2,1,0:T(8,128)(2,1)S(1)} %shard_map.59), channel_id=1, replica_groups={{169,8,0,12,16,72,200,13,4,20,24,56,64,76,80,136,192,204,208,5,9,21,77,..., dimensions={0} | all-to-all | bytes 524288 | tf_op jit(solution)/shard_map/all_to_all | solution.py:43
  53.8 1.1 %shard_map.60 = bf16[4,256,128]{2,1,0:T(8,128)(2,1)} custom-call(bf16[128,8,128]{2,1,0:T(8,128)(2,1)S(1)} %all_to_all.11.returned_ref, f32[1024,128]{1,0:T(8,128)S(1)} %get-tuple-element.19.gating_ref, bf16[128,128]{1,0:T(8,128)(2,1)S(1)} %get-tuple-element.20.out_ref), custom_call_target="tpu_custom_call" | custom-call | tf_op jit(solution)/shard_map/pallas_call | solution.py:270
Async XLA Ops:
  0.0 1.1 %copy-start = (bf16[4,256,128]{2,1,0:T(8,128)(2,1)S(1)}, bf16[4,256,128]{2,1,0:T(8,128)(2,1)}, u32[]{:S(2)}) copy-start(bf16[4,256,128]{2,1,0:T(8,128)(2,1)} %pair_ref.1) | copy-start | bytes 786436
  31.3 2.9 %collective-permute-start = (bf16[128,4,256]{2,1,0:T(4,128)(2,1)S(1)}, bf16[128,4,256]{2,1,0:T(4,128)(2,1)S(1)}, u32[]{:S(2)}, u32[]{:S(2)}) collective-permute-start(bf16[128,4,256]{2,1,0:T(4,128)(2,1)S(1)} %slice.4), channel_id=1, source_target_pairs={{0,2},{2,0},{4,6},{6,4},{8,10},{10,8},{12,14},{14,12},{16,18},{18,... | collective-permute-start | bytes 786440 | tf_op jit(solution)/shard_map/ppermute | solution.py:296

commit v11 on v10

--- a/solution.py
+++ b/solution.py
@@ -155,8 +155,8 @@
         proj = dot_rows(turned_ref[...], normed_ref[pl.ds(row * cols, cols), :])
         left = sigmoid(proj[:hidden]) * proj[hidden : 2 * hidden] * mask
         right = sigmoid(proj[2 * hidden : 3 * hidden]) * proj[3 * hidden :] * mask
-        held[row] = left.astype(jnp.bfloat16)
-        held[rows + row] = right.astype(jnp.bfloat16)
+        held[rows + row] = left.astype(jnp.bfloat16)
+        held[row] = right.astype(jnp.bfloat16)
     step = 16
     for first_channel in range(0, hidden, step):
         part = slice(first_channel, first_channel + step)
@@ -186,8 +186,8 @@
     for half in range(2):
         part = seats[half * chips : (half + 1) * chips]
         got = jnp.stack([got_ref[seat] for seat in part])
-        left_ref[half] = flat(got[:, :rows, :])
-        own_ref[half] = got[:, rows:, :].astype(jnp.float32)
+        left_ref[half] = flat(got[:, rows:, :])
+        own_ref[half] = got[:, :rows, :].astype(jnp.float32)
     gating_ref[...] = sigmoid(
         jnp.dot(normed_ref[...], gate_ref[...], preferred_element_type=jnp.float32)
     )
@@ -293,7 +293,7 @@
         normed = norm_pair(pair, share)
         sent = project_blocks(normed, valid, turned, rows, w_out.shape[0])
         got = exchange(sent, groups)
-        other = lax.ppermute(got[:, rows:, :], "wide", [(i, i ^ 1) for i in range(wide)])
+        other = lax.ppermute(got[:, :rows, :], "wide", [(i, i ^ 1) for i in range(wide)])
         left, own, gating = own_part(seats, got, normed, w_gate)
         returned = exchange(plane_blocks(seats, other, left, own), groups)
         return finish(returned, gating, w_out, pair.shape)

time: 55 us -> 54.9 us (level)
  no operation moved by 1% of the time
where the time goes in v11:
time: 54.9 us; the launch traced here: 54.8 us
  blocking collectives  48.3 us (88%)
  Pallas kernels  3.79 us (7%)
  starting transfers between devices  1.71 us (3%)
  waiting for transfers between devices  0.78 us (1%)
    all_to_all x2, blocking collectives, exchange(): lax.all_to_all(blocks, ('wide', 'row'), split_axis=0, concat_axis=0, tile...  48.3 us
    ppermute x1, starting transfers between devices, shards(): lax.ppermute(got[:, :rows, :], 'wide', [(i, i ^ 1) for i in range(wide)])  1.71 us
  transfers between devices with their start and end apart: 1, of which 1 were waited for; matrix products, arithmetic and copies ran while one was open for 0% of the time, Pallas kernels for 1%

profile of v11, /device:TPU:1, one launch (start us, length us, event | category | flops | bytes accessed | tf_op | source)
XLA Modules:
  0.0 54.8 jit_solution(15241083924635861851)
XLA Ops:
  0.0 0.0 copy-start
  0.0 1.0 %shard_map.55 = (bf16[256,128]{1,0:T(8,128)(2,1)S(1)}, bf16[512,128]{1,0:T(8,128)(2,1)S(1)}, s32[1,512]{1,0:T(1,128)S(1)}, bf16[128,128]{1,0:T(8,128)(2,1)S(1)}, bf16[128,128]{1,0:T(8,128)(2,1)S(1)}) custom-call(bf16[128,512]{1,0:T(8,128)(2,1)} %w_hbm.1, s32[1,512]{1,0:T(1,128)} %bitcast.1, bf16[128,128]{1,0:T(8,128)(2,1)} %gate_hbm.1, bf16[128,128]{1,0:T(8,128)(2,1)} %out_hbm.1), custom_call_target="tpu_custom_call" | custom-call | flops 1073741824 | bytes 8388608 | tf_op jit(solution)/shard_map/pallas_call | solution.py:83
  1.0 0.0 copy-done
  1.1 0.4 shard_map.56.normed_ref
  1.5 0.6 %shard_map.57 = bf16[128,8,256]{2,1,0:T(8,128)(2,1)S(1)} custom-call(bf16[1024,128]{1,0:T(8,128)(2,1)S(1)} %shard_map.56.normed_ref, s32[1,512]{1,0:T(1,128)S(1)} %get-tuple-element.14.valid_ref, bf16[512,128]{1,0:T(8,128)(2,1)S(1)} %get-tuple-element.15.turned_ref), custom_call_target="tpu_custom_call" | custom-call | tf_op jit(solution)/shard_map/pallas_call | solution.py:168
  2.1 29.1 %all_to_all.10.got_ref = bf16[128,8,256]{2,1,0:T(8,128)(2,1)S(1)} all-to-all(bf16[128,8,256]{2,1,0:T(8,128)(2,1)S(1)} %shard_map.57), channel_id=1, replica_groups={{169,8,0,12,16,72,200,13,4,20,24,56,64,76,80,136,192,204,208,5,9,21,77,..., dimensions={0} | all-to-all | bytes 1048576 | tf_op jit(solution)/shard_map/all_to_all | solution.py:43
  31.1 0.1 slice.4
  31.2 1.7 %collective-permute-start = (bf16[128,4,256]{2,1,0:T(4,128)(2,1)S(1)}, bf16[128,4,256]{2,1,0:T(4,128)(2,1)S(1)}, u32[]{:S(2)}, u32[]{:S(2)}) collective-permute-start(bf16[128,4,256]{2,1,0:T(4,128)(2,1)S(1)} %slice.4), channel_id=1, source_target_pairs={{0,2},{2,0},{4,6},{6,4},{8,10},{10,8},{12,14},{14,12},{16,18},{18,... | collective-permute-start | bytes 786440 | tf_op jit(solution)/shard_map/ppermute | solution.py:296
  32.9 0.4 shard_map.58
  33.3 0.8 %collective-permute-done.other_ref = bf16[128,4,256]{2,1,0:T(4,128)(2,1)S(1)} collective-permute-done((bf16[128,4,256]{2,1,0:T(4,128)(2,1)S(1)}, bf16[128,4,256]{2,1,0:T(4,128)(2,1)S(1)}, u32[]{:S(2)}, u32[]{:S(2)}) %collective-permute-start) | collective-permute-done | bytes 262176 | tf_op jit(solution)/shard_map/ppermute | solution.py:296
  34.1 0.4 shard_map.59
  34.5 19.3 %all_to_all.11.returned_ref = bf16[128,8,128]{2,1,0:T(8,128)(2,1)S(1)} all-to-all(bf16[128,8,128]{2,1,0:T(8,128)(2,1)S(1)} %shard_map.59), channel_id=1, replica_groups={{169,8,0,12,16,72,200,13,4,20,24,56,64,76,80,136,192,204,208,5,9,21,77,..., dimensions={0} | all-to-all | bytes 524288 | tf_op jit(solution)/shard_map/all_to_all | solution.py:43
  53.7 1.1 %shard_map.60 = bf16[4,256,128]{2,1,0:T(8,128)(2,1)} custom-call(bf16[128,8,128]{2,1,0:T(8,128)(2,1)S(1)} %all_to_all.11.returned_ref, f32[1024,128]{1,0:T(8,128)S(1)} %get-tuple-element.19.gating_ref, bf16[128,128]{1,0:T(8,128)(2,1)S(1)} %get-tuple-element.20.out_ref), custom_call_target="tpu_custom_call" | custom-call | tf_op jit(solution)/shard_map/pallas_call | solution.py:270
Async XLA Ops:
  0.0 1.1 %copy-start = (bf16[4,256,128]{2,1,0:T(8,128)(2,1)S(1)}, bf16[4,256,128]{2,1,0:T(8,128)(2,1)}, u32[]{:S(2)}) copy-start(bf16[4,256,128]{2,1,0:T(8,128)(2,1)} %pair_ref.1) | copy-start | bytes 786436
  31.2 2.9 %collective-permute-start = (bf16[128,4,256]{2,1,0:T(4,128)(2,1)S(1)}, bf16[128,4,256]{2,1,0:T(4,128)(2,1)S(1)}, u32[]{:S(2)}, u32[]{:S(2)}) collective-permute-start(bf16[128,4,256]{2,1,0:T(4,128)(2,1)S(1)} %slice.4), channel_id=1, source_target_pairs={{0,2},{2,0},{4,6},{6,4},{8,10},{10,8},{12,14},{14,12},{16,18},{18,... | collective-permute-start | bytes 786440 | tf_op jit(solution)/shard_map/ppermute | solution.py:296

commit v12 on v9

--- a/solution.py
+++ b/solution.py
@@ -137,14 +137,16 @@
     seat = lax.broadcasted_iota(jnp.int32, valid.shape, 1)
     first = lax.axis_index("wide") * rows
     col_valid = jnp.where(lax.axis_index("row") == 0, valid[:, :cols], valid[:, cols:])
-    for row in range(rows):
-        row_valid = jnp.sum(jnp.where(seat == first + row, valid, 0.0), axis=1, keepdims=True)
-        mask = row_valid * col_valid
-        proj = dot_rows(turned_ref[...], normed_ref[pl.ds(row * cols, cols), :])
-        left = sigmoid(proj[:hidden]) * proj[hidden : 2 * hidden] * mask
-        right = sigmoid(proj[2 * hidden : 3 * hidden]) * proj[3 * hidden :] * mask
-        held[row] = left.astype(jnp.bfloat16)
-        held[rows + row] = right.astype(jnp.bfloat16)
+    for side in range(2):
+        gate_rows = pl.ds(2 * side * hidden, hidden)
+        value_rows = pl.ds((2 * side + 1) * hidden, hidden)
+        for row in range(rows):
+            row_valid = jnp.sum(jnp.where(seat == first + row, valid, 0.0), axis=1, keepdims=True)
+            normed = normed_ref[pl.ds(row * cols, cols), :]
+            gate = sigmoid(dot_rows(turned_ref[gate_rows, :], normed))
+            value = dot_rows(turned_ref[value_rows, :], normed)
+            mask = row_valid * col_valid
+            held[side * rows + row] = (gate * value * mask).astype(jnp.bfloat16)
     step = 16
     for first_channel in range(0, hidden, step):
         part = slice(first_channel, first_channel + step)

time: 55 us -> 55 us (level)
  no operation moved by 1% of the time
where the time goes in v12:
time: 55 us; the launch traced here: 54.8 us
  blocking collectives  48.3 us (88%)
  Pallas kernels  3.77 us (7%)
  starting transfers between devices  1.71 us (3%)
  waiting for transfers between devices  0.77 us (1%)
    all_to_all x2, blocking collectives, exchange(): lax.all_to_all(blocks, ('wide', 'row'), split_axis=0, concat_axis=0, tile...  48.3 us
    ppermute x1, starting transfers between devices, shards(): lax.ppermute(got[:, rows:, :], 'wide', [(i, i ^ 1) for i in range(wide)])  1.71 us
  transfers between devices with their start and end apart: 1, of which 1 were waited for; matrix products, arithmetic and copies ran while one was open for 0% of the time, Pallas kernels for 1%

profile of v12, /device:TPU:1, one launch (start us, length us, event | category | flops | bytes accessed | tf_op | source)
XLA Modules:
  0.0 54.8 jit_solution(17948588976559066653)
XLA Ops:
  0.0 0.0 copy-start
  0.0 1.0 %shard_map.55 = (bf16[256,128]{1,0:T(8,128)(2,1)S(1)}, bf16[512,128]{1,0:T(8,128)(2,1)S(1)}, s32[1,512]{1,0:T(1,128)S(1)}) custom-call(bf16[128,512]{1,0:T(8,128)(2,1)} %w_hbm.1, s32[1,512]{1,0:T(1,128)} %bitcast.1), custom_call_target="tpu_custom_call" | custom-call | flops 1073741824 | bytes 8388608 | tf_op jit(solution)/shard_map/pallas_call | solution.py:78
  1.0 0.0 copy-done
  1.0 0.4 shard_map.56.normed_ref
  1.5 0.6 %shard_map.57 = bf16[128,8,256]{2,1,0:T(8,128)(2,1)S(1)} custom-call(bf16[1024,128]{1,0:T(8,128)(2,1)S(1)} %shard_map.56.normed_ref, s32[1,512]{1,0:T(1,128)S(1)} %get-tuple-element.13.valid_ref, bf16[512,128]{1,0:T(8,128)(2,1)S(1)} %get-tuple-element.14.turned_ref), custom_call_target="tpu_custom_call" | custom-call | tf_op jit(solution)/shard_map/pallas_call | solution.py:158
  2.0 29.1 %all_to_all.10.got_ref = bf16[128,8,256]{2,1,0:T(8,128)(2,1)S(1)} all-to-all(bf16[128,8,256]{2,1,0:T(8,128)(2,1)S(1)} %shard_map.57), channel_id=1, replica_groups={{169,8,0,12,16,72,200,13,4,20,24,56,64,76,80,136,192,204,208,5,9,21,77,..., dimensions={0} | all-to-all | bytes 1048576 | tf_op jit(solution)/shard_map/all_to_all | solution.py:43
  31.1 0.0 copy-start.1
  31.1 0.0 copy-start.2
  31.1 0.1 slice.4
  31.3 1.7 %collective-permute-start = (bf16[128,4,256]{2,1,0:T(4,128)(2,1)S(1)}, bf16[128,4,256]{2,1,0:T(4,128)(2,1)S(1)}, u32[]{:S(2)}, u32[]{:S(2)}) collective-permute-start(bf16[128,4,256]{2,1,0:T(4,128)(2,1)S(1)} %slice.4), channel_id=1, source_target_pairs={{0,2},{2,0},{4,6},{6,4},{8,10},{10,8},{12,14},{14,12},{16,18},{18,... | collective-permute-start | bytes 786440 | tf_op jit(solution)/shard_map/ppermute | solution.py:288
  33.0 0.0 copy-done.1
  33.0 0.0 copy-done.2
  33.0 0.4 shard_map.58
  33.4 0.8 %collective-permute-done.other_ref = bf16[128,4,256]{2,1,0:T(4,128)(2,1)S(1)} collective-permute-done((bf16[128,4,256]{2,1,0:T(4,128)(2,1)S(1)}, bf16[128,4,256]{2,1,0:T(4,128)(2,1)S(1)}, u32[]{:S(2)}, u32[]{:S(2)}) %collective-permute-start) | collective-permute-done | bytes 262176 | tf_op jit(solution)/shard_map/ppermute | solution.py:288
  34.1 0.4 shard_map.59
  34.5 19.3 %all_to_all.11.returned_ref = bf16[128,8,128]{2,1,0:T(8,128)(2,1)S(1)} all-to-all(bf16[128,8,128]{2,1,0:T(8,128)(2,1)S(1)} %shard_map.59), channel_id=1, replica_groups={{169,8,0,12,16,72,200,13,4,20,24,56,64,76,80,136,192,204,208,5,9,21,77,..., dimensions={0} | all-to-all | bytes 524288 | tf_op jit(solution)/shard_map/all_to_all | solution.py:43
  53.8 1.1 %shard_map.60 = bf16[4,256,128]{2,1,0:T(8,128)(2,1)} custom-call(bf16[128,8,128]{2,1,0:T(8,128)(2,1)S(1)} %all_to_all.11.returned_ref, f32[1024,128]{1,0:T(8,128)S(1)} %get-tuple-element.17.gating_ref, bf16[128,128]{1,0:T(8,128)(2,1)S(1)} %get-tuple-element.18.out_ref), custom_call_target="tpu_custom_call" | custom-call | tf_op jit(solution)/shard_map/pallas_call | solution.py:264
Async XLA Ops:
  0.0 1.0 %copy-start = (bf16[4,256,128]{2,1,0:T(8,128)(2,1)S(1)}, bf16[4,256,128]{2,1,0:T(8,128)(2,1)}, u32[]{:S(2)}) copy-start(bf16[4,256,128]{2,1,0:T(8,128)(2,1)} %pair_ref.1) | copy-start | bytes 786436
  31.1 1.9 %copy-start.1 = (bf16[128,128]{1,0:T(8,128)(2,1)S(1)}, bf16[128,128]{1,0:T(8,128)(2,1)}, u32[]{:S(2)}) copy-start(bf16[128,128]{1,0:T(8,128)(2,1)} %gate_ref.1) | copy-start | bytes 98308
  31.1 1.9 %copy-start.2 = (bf16[128,128]{1,0:T(8,128)(2,1)S(1)}, bf16[128,128]{1,0:T(8,128)(2,1)}, u32[]{:S(2)}) copy-start(bf16[128,128]{1,0:T(8,128)(2,1)} %w_out_ref.1) | copy-start | bytes 98308
  31.3 2.9 %collective-permute-start = (bf16[128,4,256]{2,1,0:T(4,128)(2,1)S(1)}, bf16[128,4,256]{2,1,0:T(4,128)(2,1)S(1)}, u32[]{:S(2)}, u32[]{:S(2)}) collective-permute-start(bf16[128,4,256]{2,1,0:T(4,128)(2,1)S(1)} %slice.4), channel_id=1, source_target_pairs={{0,2},{2,0},{4,6},{6,4},{8,10},{10,8},{12,14},{14,12},{16,18},{18,... | collective-permute-start | bytes 786440 | tf_op jit(solution)/shard_map/ppermute | solution.py:288
